TPU v7x, 32 devices: a whole 2x2x4 slice. The times are simulated.
32 devices in a mesh: dp: 8 (over y, x, core), cross: 4 (over z).
Axes of the slice: x: 2, y: 2, z: 4, core: 2. Of those that a mesh axis runs over, the one named last changes fastest.
Arguments:
- emb_table: bfloat16 [4096, 1014], P('cross'), may hold values from -6 to 6
- dense_input: bfloat16 [8192, 13], P('dp'), may hold values from -6 to 6
- feature_ids: int32 [8192, 26], P('dp'), may hold values from 0 to 4095
- labels: int32 [8192], P(('dp', 'cross')), may hold values 0 or 1
- cross_weight: bfloat16 [3, 1040, 1040], P(None, 'cross'), may hold values from -0.1875 to 0.1875
- cross_bias: bfloat16 [3, 1040], P(None, 'cross'), may hold values from -3 to 3
- tower_one: bfloat16 [1040, 1024], replicated, may hold values from -0.1875 to 0.1875
- bias_one: float32 [1024], replicated, may hold values from -3 to 3
- tower_two: bfloat16 [1024, 1024], replicated, may hold values from -0.1875 to 0.1875
- bias_two: float32 [1024], replicated, may hold values from -3 to 3
- out_weight: bfloat16 [2064], replicated, may hold values from -0.125 to 0.125
- out_bias: float32 [1], replicated, may hold values from -3 to 3
Outputs:
- loss_value: float32 [], replicated
- logits: float32 [8192], P(('dp', 'cross'))
- dense_grad: float32 [8192, 13], P(('dp', 'cross'))
- table_grad: float32 [4096, 1014], P('cross')
- cross_weight_grad: float32 [3, 1040, 1040], P(None, 'cross')
- cross_bias_grad: float32 [3, 1040], P(None, 'cross')
- tower_one_grad: float32 [1040, 1024], replicated
- bias_one_grad: float32 [1024], replicated
- tower_two_grad: float32 [1024, 1024], replicated
- bias_two_grad: float32 [1024], replicated
- out_weight_grad: float32 [2064], replicated
- out_bias_grad: float32 [1], replicated
- row_counts: int32 [4096, 26], P('cross')
All inputs are finite; a program needn't handle non-finite values. No bound on the sum of `labels` on one device may be relied on, other than what follows from the above.
Results may differ from a plain program's by a relative error of at most 0.008.
Values may be sent and summed in bfloat16 or wider, within the bound.
No kernel may reach another device: no remote copies, remote signals or barrier semaphores. Data moves between devices by JAX's collectives and lax.ppermute only.
A program may use at most 128 MiB of HBM per device.

v0:
```python
import jax
import jax.numpy as jnp
from jax import lax
from jax.sharding import PartitionSpec as P

contract_first = (((0,), (0,)), ((), ()))
contract_last = (((1,), (1,)), ((), ()))
contract_cross = (((1,), (0,)), ((), ()))
contract_outer = (((0,), (1,)), ((), ()))
exact_mode = lax.Precision.HIGHEST


def silu_slope(pre_act):
    sigmoid_part = jax.nn.sigmoid(pre_act)
    return sigmoid_part * (1.0 + pre_act * (1.0 - sigmoid_part))


def field_hot(id_rows, field_index, first_row, rows_here, hot_type):
    local_ids = lax.dynamic_slice_in_dim(id_rows, field_index, 1, 1)[:, 0] - first_row
    return (local_ids[:, None] == jnp.arange(rows_here, dtype=jnp.int32)[None, :]).astype(hot_type)


def lookup_term(emb_table, id_rows, first_row, emb_width, full_width):
    rows_here = emb_table.shape[0]
    row_count, fields = id_rows.shape

    def lookup_add_field(field_index, looked):
        hot_rows = field_hot(id_rows, field_index, first_row, rows_here, jnp.bfloat16)
        table_cols = lax.dynamic_slice_in_dim(emb_table, field_index * emb_width, emb_width, 1)
        picked = lax.dot_general(
            table_cols, hot_rows, contract_outer, preferred_element_type=jnp.float32
        )
        return lax.dynamic_update_slice_in_dim(looked, picked, field_index * emb_width, 0)

    looked = lax.fori_loop(
        0, fields, lookup_add_field, jnp.zeros((fields * emb_width, row_count), jnp.float32)
    )
    padding = jnp.zeros((full_width - fields * emb_width, row_count), jnp.float32)
    return jnp.concatenate([looked, padding], axis=0)


def dense_columns(dense_rows, emb_end, full_width):
    row_count, dense_width = dense_rows.shape
    before = jnp.zeros((emb_end, row_count), jnp.float32)
    after = jnp.zeros((full_width - emb_end - dense_width, row_count), jnp.float32)
    return jnp.concatenate([before, dense_rows.astype(jnp.float32).T, after], axis=0)


def table_terms(rows_here, first_row, id_rows, emb_grad, emb_width):
    row_count, fields = id_rows.shape
    ones_row = jnp.ones((1, row_count), jnp.float32)

    def table_add_field(field_index, carry_pair):
        grad_table, count_table = carry_pair
        hot_rows = field_hot(id_rows, field_index, first_row, rows_here, jnp.float32)
        piece = lax.dynamic_slice_in_dim(emb_grad, field_index * emb_width, emb_width, 0)
        piece = jnp.concatenate([piece, ones_row], axis=0)
        summed = lax.dot_general(
            hot_rows,
            piece,
            contract_outer,
            precision=exact_mode,
            preferred_element_type=jnp.float32,
        )
        grad_table = lax.dynamic_update_slice_in_dim(
            grad_table, summed[:, :emb_width], field_index * emb_width, 1
        )
        count_table = lax.dynamic_update_slice_in_dim(
            count_table, summed[:, emb_width:], field_index, 1
        )
        return (grad_table, count_table)

    start_pair = (
        jnp.zeros((rows_here, fields * emb_width), jnp.float32),
        jnp.zeros((rows_here, fields), jnp.float32),
    )
    return lax.fori_loop(0, fields, table_add_field, start_pair)


def body(
    emb_table,
    dense_input,
    feature_ids,
    labels,
    cross_weight,
    cross_bias,
    tower_one,
    bias_one,
    tower_two,
    bias_two,
    out_weight,
    out_bias,
):
    layer_count, shard_width, full_width = cross_weight.shape
    fields = feature_ids.shape[1]
    emb_width = emb_table.shape[1] // fields
    dense_width = dense_input.shape[1]
    cross_ways = lax.axis_size("cross")
    cross_place = lax.axis_index("cross")
    all_rows = feature_ids.shape[0]
    row_count = all_rows // cross_ways
    row_start = cross_place * row_count
    example_total = row_count * lax.axis_size("dp") * cross_ways
    emb_end = fields * emb_width
    rows_here = emb_table.shape[0]
    first_row = cross_place * rows_here
    term_cols = lookup_term(emb_table, feature_ids, first_row, emb_width, full_width)
    low_states = []
    mix_terms = []
    emb_shard = lax.psum_scatter(
        term_cols.astype(jnp.bfloat16), "cross", scatter_dimension=0, tiled=True
    ).astype(jnp.float32)
    dense_shard = lax.dynamic_slice_in_dim(
        dense_columns(dense_input, emb_end, full_width), cross_place * shard_width, shard_width, 0
    )
    first_input = emb_shard + dense_shard
    cross_state = first_input
    for layer_index in range(layer_count):
        low_state = cross_state.astype(jnp.bfloat16)
        layer_weight = cross_weight[layer_index]

        def product_rows(begin_row, count_rows, low_state=low_state, layer_weight=layer_weight):
            return lax.dot_general(
                layer_weight, low_state, contract_first, preferred_element_type=jnp.float32
            )

        summed = lax.psum_scatter(
            product_rows(jnp.int32(0), shard_width * lax.axis_size("cross")),
            "cross",
            scatter_dimension=0,
            tiled=True,
        )
        mixed_term = summed + cross_bias[layer_index].astype(jnp.float32)[:, None]
        low_states.append(low_state)
        mix_terms.append(mixed_term)
        cross_state = first_input * mixed_term + cross_state
    top_values = lax.all_to_all(
        cross_state.astype(jnp.bfloat16), "cross", split_axis=1, concat_axis=0, tiled=True
    )
    label_values = labels.astype(jnp.float32)
    hid_one = (
        lax.dot_general(top_values, tower_one, contract_first, preferred_element_type=jnp.float32)
        + bias_one[None, :]
    )
    act_one = jax.nn.silu(hid_one).astype(jnp.bfloat16)
    hid_two = jnp.dot(act_one, tower_two, preferred_element_type=jnp.float32) + bias_two[None, :]
    act_two = jax.nn.silu(hid_two).astype(jnp.bfloat16)
    logits = (
        lax.dot_general(
            top_values, out_weight[:full_width], contract_first, preferred_element_type=jnp.float32
        )
        + jnp.dot(act_two, out_weight[full_width:], preferred_element_type=jnp.float32)
        + out_bias[0]
    )
    loss_part = jnp.sum(jax.nn.softplus(logits) - label_values * logits) / example_total
    logit_grad = ((jax.nn.sigmoid(logits) - label_values) / example_total).astype(jnp.bfloat16)
    logit_float = logit_grad.astype(jnp.float32)
    out_grad = jnp.concatenate(
        [
            lax.dot_general(
                top_values, logit_grad, contract_cross, preferred_element_type=jnp.float32
            ),
            lax.dot_general(
                act_two, logit_grad, contract_first, preferred_element_type=jnp.float32
            ),
        ]
    )
    out_bias_grad = jnp.sum(logit_float).reshape(1)
    grad_two = (
        logit_float[:, None]
        * out_weight[full_width:].astype(jnp.float32)[None, :]
        * silu_slope(hid_two)
    ).astype(jnp.bfloat16)
    tower_two_grad = lax.dot_general(
        act_one, grad_two, contract_first, preferred_element_type=jnp.float32
    )
    bias_two_grad = jnp.sum(grad_two.astype(jnp.float32), axis=0)
    grad_one = (
        lax.dot_general(grad_two, tower_two, contract_last, preferred_element_type=jnp.float32)
        * silu_slope(hid_one)
    ).astype(jnp.bfloat16)
    tower_one_grad = jnp.dot(top_values, grad_one, preferred_element_type=jnp.float32)
    bias_one_grad = jnp.sum(grad_one.astype(jnp.float32), axis=0)
    top_grad = (
        lax.dot_general(tower_one, grad_one, contract_last, preferred_element_type=jnp.float32)
        + out_weight[:full_width].astype(jnp.float32)[:, None] * logit_float[None, :]
    ).astype(jnp.bfloat16)
    tower_sums = lax.psum(
        (
            loss_part,
            tower_one_grad,
            bias_one_grad,
            tower_two_grad,
            bias_two_grad,
            out_grad,
            out_bias_grad,
        ),
        ("dp", "cross"),
    )
    weight_grads = [None] * layer_count
    bias_grads = [None] * layer_count
    grad_state = lax.all_to_all(top_grad, "cross", split_axis=0, concat_axis=1, tiled=True).astype(
        jnp.float32
    )
    input_grad = jnp.zeros_like(first_input)
    for layer_index in reversed(range(layer_count)):
        mixed_grad = (grad_state * first_input).astype(jnp.bfloat16)
        bias_grads[layer_index] = jnp.sum(mixed_grad.astype(jnp.float32), axis=1)
        input_grad = input_grad + grad_state * mix_terms[layer_index]

        def fold_rows(
            carry_pair,
            piece_rows,
            begin_row,
            low_state=low_states[layer_index],
            layer_weight=cross_weight[layer_index],
        ):
            block_term = lax.dot_general(
                low_state, piece_rows, contract_last, preferred_element_type=jnp.float32
            )
            back_part = jnp.dot(layer_weight, piece_rows, preferred_element_type=jnp.float32)
            return (block_term, back_part)

        start_pair = (jnp.zeros((shard_width, full_width), jnp.float32), jnp.zeros_like(grad_state))
        weight_grads[layer_index], back_term = fold_rows(
            start_pair, lax.all_gather(mixed_grad, "cross", axis=0, tiled=True), jnp.int32(0)
        )
        grad_state = grad_state + back_term
    input_grad = input_grad + grad_state
    full_grad = lax.all_gather(input_grad, "cross", axis=0, tiled=True)
    dense_block = lax.dynamic_slice_in_dim(
        full_grad[emb_end : emb_end + dense_width], row_start, row_count, 1
    )
    dense_grad = dense_block.T
    table_term, count_term = table_terms(
        rows_here, first_row, feature_ids, full_grad[:emb_end], emb_width
    )
    cross_pair = (jnp.stack(weight_grads), jnp.stack(bias_grads))
    cross_weight_grad, cross_bias_grad = lax.psum((cross_pair[0], cross_pair[1]), "dp")
    table_share, count_share = (
        lax.psum_scatter(table_term, "dp", scatter_dimension=0, tiled=True),
        lax.psum_scatter(count_term, "dp", scatter_dimension=0, tiled=True),
    )
    table_grad, count_sum = (
        lax.all_gather(table_share, "dp", axis=0, tiled=True),
        lax.all_gather(count_share, "dp", axis=0, tiled=True),
    )
    return (
        tower_sums[0],
        logits,
        dense_grad,
        table_grad,
        cross_weight_grad,
        cross_bias_grad,
        tower_sums[1],
        tower_sums[2],
        tower_sums[3],
        tower_sums[4],
        tower_sums[5],
        tower_sums[6],
        count_sum.astype(jnp.int32),
    )


def solution(mesh):
    in_specs = (
        P("cross", None),
        P("dp", None),
        P("dp", None),
        P(("dp", "cross")),
        P(None, "cross", None),
        P(None, "cross"),
        P(),
        P(),
        P(),
        P(),
        P(),
        P(),
    )
    out_specs = (
        P(),
        P(("dp", "cross")),
        P(("dp", "cross"), None),
        P("cross", None),
        P(None, "cross", None),
        P(None, "cross"),
        P(),
        P(),
        P(),
        P(),
        P(),
        P(),
        P("cross", None),
    )
    return jax.shard_map(body, mesh=mesh, in_specs=in_specs, out_specs=out_specs, check_vma=False)
```

profile of v0, /device:TPU:13, one launch (start us, length us, event | category | flops | bytes accessed | tf_op | source)
XLA Modules:
  0.0 1290.4 jit_solution(7958234236842441129)
XLA Ops:
  9.6 111.5 %while.28 = (s32[]{:T(128)}, bf16[1014,1024]{1,0:T(8,128)(2,1)}, bf16[1024,1014]{0,1:T(8,128)(2,1)}, s32[1024,26]{0,1:T(8,128)}, s32[]{:T(128)}, /*index=5*/s32[]{:T(128)}, s32[]{:T(128)}, s32[]{:T(128)}, s32[]{:T(128)}) while((s32[]{:T(128)}, bf16[1014,1024]{1,0:T(8,128)(2,1)}, bf16[1024,1014]{0,1:T(8,128)(2,1)}, s32[1024,26]{0,1:T(8,128)}, ...), condition=%wide.region_1.0_spmd, body=%wide.region_0.0_spmd.sunk | while | flops 82838536 | bytes 333987 | solution.py:35
  10.4 1.9 fusion.75
  40.4 1.9 fusion.75
  53.3 1.9 fusion.75
  57.5 1.9 fusion.75
  66.1 1.9 fusion.75
  91.9 1.9 fusion.75
  117.6 1.9 fusion.75
  121.1 3.1 concatenate.14
  124.2 41.2 %fusion = bf16[264,1024]{1,0:T(8,128)(2,1)S(1)} fusion(bf16[1040,1024]{1,0:T(8,128)(2,1)} %concatenate.14), kind=kCustom, calls=%all-reduce-scatter | all-reduce-scatter fusion | flops 1081345 | bytes 2671104
  165.5 2.2 collective-permute-start
  168.9 2.5 broadcast.27
  171.5 13.0 %concatenate.15 = f32[1040,1024]{1,0:T(8,128)} concatenate(f32[1014,1024]{1,0:T(8,128)} %broadcast.27, f32[13,1024]{1,0:T(8,128)S(1)} %convert_bitcast_fusion.1, f32[13,1024]{1,0:T(8,128)S(1)} %broadcast_in_dim.18), dimensions={0} | concatenate | bytes 8519680 | tf_op jit(solution)/shard_map/concatenate | solution.py:46
  184.4 3.6 concatenate.17
  189.7 4.4 convolution_bitcast_fusion.2
  194.1 75.3 %fusion.1 = f32[264,1024]{1,0:T(8,128)} fusion(f32[1040,1024]{1,0:T(8,128)} %convolution_bitcast_fusion.2), kind=kCustom, calls=%all-reduce-scatter.1 | all-reduce-scatter fusion | flops 1081345 | bytes 5341696
  270.2 1.9 collective-permute-start.1
  272.2 3.0 collective-permute-done.1
  275.2 4.6 concatenate.18
  282.1 4.4 convolution_bitcast_fusion.1
  286.5 72.2 %fusion.2 = f32[264,1024]{1,0:T(8,128)} fusion(f32[1040,1024]{1,0:T(8,128)} %convolution_bitcast_fusion.1), kind=kCustom, calls=%all-reduce-scatter.2 | all-reduce-scatter fusion | flops 1081345 | bytes 5341696
  359.6 3.7 collective-permute-start.2
  364.6 4.6 concatenate.19
  369.2 2.0 multiply_add_fusion.1
  372.2 4.4 convolution_bitcast_fusion
  376.6 72.6 %fusion.3 = f32[264,1024]{1,0:T(8,128)} fusion(f32[1040,1024]{1,0:T(8,128)} %convolution_bitcast_fusion), kind=kCustom, calls=%all-reduce-scatter.3 | all-reduce-scatter fusion | flops 1081345 | bytes 5341696
  450.1 4.1 collective-permute-start.3
  455.5 4.6 concatenate.20
  460.1 2.6 add_convert_fusion
  462.7 2.4 all_to_all.24
  465.1 1.9 copy.28
  467.1 4.3 all-to-all-start
  472.2 7.0 all-to-all-done
  479.2 1.9 all_to_all.27
  482.4 2.1 convolution_add_fusion.1
  492.0 12.4 all_to_all.32
  506.4 53.2 %all-gather.12.cloned.1.call-done = bf16[4,260,1024]{2,1,0:T(8,128)(2,1)} async-done(((bf16[1,260,1024]{2,1,0:T(8,128)(2,1)}), bf16[4,260,1024]{2,1,0:T(8,128)(2,1)}) %all-gather.12.cloned.1.call-update) | async-done | bytes 2129936 | tf_op jit(solution)/shard_map/all_gather | solution.py:226
  559.5 2.8 reshape.70
  562.3 3.7 convert_reduce_fusion.1
  566.1 46.1 %all-gather.14.cloned.1.call-done = bf16[4,260,1024]{2,1,0:T(8,128)(2,1)} async-done(((bf16[1,260,1024]{2,1,0:T(8,128)(2,1)}), bf16[4,260,1024]{2,1,0:T(8,128)(2,1)}) %all-gather.14.cloned.1.call-update) | async-done | bytes 2129936 | tf_op jit(solution)/shard_map/all_gather | solution.py:226
  612.2 2.8 reshape.72
  615.0 4.1 convert_reduce_fusion.2
  619.1 46.1 %all-gather.16.cloned.1.call-done = bf16[4,260,1024]{2,1,0:T(8,128)(2,1)} async-done(((bf16[1,260,1024]{2,1,0:T(8,128)(2,1)}), bf16[4,260,1024]{2,1,0:T(8,128)(2,1)}) %all-gather.16.cloned.1.call-update) | async-done | bytes 2129936 | tf_op jit(solution)/shard_map/all_gather | solution.py:226
  665.2 2.8 reshape.74
  668.0 5.6 add_bitcast_fusion
  673.7 81.4 %all-gather.18.cloned.1.call-done = f32[4,260,1024]{2,1,0:T(8,128)} async-done(((f32[1,260,1024]{2,1,0:T(8,128)}), f32[4,260,1024]{2,1,0:T(8,128)}) %all-gather.18.cloned.1.call-update) | async-done | bytes 4259856 | tf_op jit(solution)/shard_map/all_gather | solution.py:230
  755.1 3.8 reshape.76
  758.9 4.8 slice.62
  763.7 2.5 broadcast_in_dim.19
  766.2 168.9 %while.29 = (s32[]{:T(128)}, f32[1024,1014]{0,1:T(8,128)}, f32[1024,26]{0,1:T(8,128)}, s32[1024,26]{0,1:T(8,128)}, s32[]{:T(128)}, /*index=5*/f32[1014,1024]{1,0...) while((s32[]{:T(128)}, f32[1024,1014]{0,1:T(8,128)}, f32[1024,26]{0,1:T(8,128)}, s32[1024,26]{0,1:T(8,128)}, ...), condition=%wide.region_9.10_spmd, body=%wide.region_8.9_spmd.sunk | while | flops 504366080 | bytes 991407 | solution.py:77
  935.7 53.3 %reduce-scatter.11.cloned.1.call-done = f32[128,1014]{0,1:T(8,128)} async-done(((f32[1024,1014]{0,1:T(8,128)}), f32[128,1014]{0,1:T(8,128)}) %reduce-scatter.11.cloned.1.call-update) | async-done | bytes 519184 | tf_op jit(solution)/shard_map/reduce_scatter | solution.py:241
  989.3 2.8 fusion.42
  992.1 2.8 fusion.39
  996.1 2.7 convolution_bitcast_fusion.3
  1001.4 2.5 pad_maximum_fusion
  1005.7 42.0 %all-reduce.10 = (f32[]{:T(128)}, f32[1024]{0:T(1024)}, f32[1024]{0:T(1024)}, f32[2064]{0:T(1024)}, f32[1]{0:T(128)}) all-reduce(f32[]{:T(128)S(6)} %div.23, f32[1024]{0:T(1024)S(1)} %get-tuple-element.269, f32[1024]{0:T(1024)S(1)} %get-tuple-element.261, ...), channel_id=1, replica_groups=mesh['dp'=8,'cross'=4] {'dp','cross'}, use_global_device_ids=true, to_apply=%region_7.8 | all-reduce | flops 4114 | bytes 32912 | tf_op jit(solution)/shard_map/psum | solution.py:188
  1047.7 14.2 %psum.65 = f32[3,260]{1,0:T(4,128)} all-reduce(f32[3,260]{1,0:T(4,128)S(1)} %pad_maximum_fusion.2), channel_id=1, replica_groups=mesh['dp'=8,'cross'=4] {'dp'}, use_global_device_ids=true, to_apply=%region_15.16 | all-reduce | flops 780 | bytes 6240 | tf_op jit(solution)/shard_map/psum | solution.py:239
  1063.5 9.3 all_gather.23
  1073.5 115.5 %all-reduce.17.cloned.1.call-done = (f32[1040,1024]{1,0:T(8,128)}, f32[1024,1024]{1,0:T(8,128)}) async-done(((f32[1040,1024]{1,0:T(8,128)}, f32[1024,1024]{1,0:T(8,128)}), (f32[1040,1024]{1,0:T(8,128)}, f32[1024,1024]{1,0:T(8,128)})) %all-reduce.17.cloned.1.call-update) | async-done | bytes 8454160 | tf_op jit(solution)/shard_map/psum | solution.py:188
  1189.0 78.7 %all-reduce.15.cloned.1.call-done = f32[3,260,1040]{2,1,0:T(8,128)} async-done(((f32[3,260,1040]{2,1,0:T(8,128)}), f32[3,260,1040]{2,1,0:T(8,128)}) %all-reduce.15.cloned.1.call-update) | async-done | bytes 3244816 | tf_op jit(solution)/shard_map/psum | solution.py:239
  1267.7 4.9 copy.54
  1272.6 1.9 copy.55
  1276.1 2.2 copy.56
  1279.9 2.1 copy.57
  (352 shorter events, 301.9 us)
Async XLA Ops:
  8.0 474.4 %copy-start = (bf16[1040,1024]{1,0:T(8,128)(2,1)S(1)}, bf16[1040,1024]{1,0:T(8,128)(2,1)}, u32[]{:S(2)}) copy-start(bf16[1040,1024]{1,0:T(8,128)(2,1)} %param.22) | copy-start | bytes 6389764
  124.2 43.5 %copy-start.20 = (bf16[1024,13]{0,1:T(8,128)(2,1)S(1)}, bf16[1024,13]{0,1:T(8,128)(2,1)}, u32[]{:S(2)}) copy-start(bf16[1024,13]{0,1:T(8,128)(2,1)} %param.17) | copy-start | bytes 79876
  124.2 43.5 %copy-start.26 = (u32[32]{0:T(128)S(1)}, u32[32]{0:T(128)}, u32[]{:S(2)}) copy-start(u32[32]{0:T(128)} %constant.116) | copy-start | bytes 388
  165.5 19.0 %collective-permute-start = (bf16[12,1024]{1,0:T(8,128)(2,1)S(1)}, bf16[12,1024]{1,0:T(8,128)(2,1)S(1)}, u32[]{:S(2)}, u32[]{:S(2)}) collective-permute-start(bf16[12,1024]{1,0:T(8,128)(2,1)S(1)} %slice.63), channel_id=1, source_target_pairs={{0,1},{1,2},{2,3},{4,5},{5,6},{6,7},{8,9},{9,10},{10,11},{12,13},{... | collective-permute-start | bytes 73736
  194.1 78.0 %copy-start.22 = (bf16[3,260]{1,0:T(4,128)(2,1)S(1)}, bf16[3,260]{1,0:T(4,128)(2,1)}, u32[]{:S(2)}) copy-start(bf16[3,260]{1,0:T(4,128)(2,1)} %param.21) | copy-start | bytes 4684
  270.2 5.0 collective-permute-start.1
  281.3 0.8 copy-start.9
  359.6 5.1 collective-permute-start.2
  371.2 1.0 copy-start.5
  450.1 5.4 collective-permute-start.3
  462.7 9.4 copy-start.23
  465.1 17.3 %copy-start.21 = (f32[1024]{0:T(1024)S(1)}, f32[1024]{0:T(1024)}, u32[]{:S(2)}) copy-start(f32[1024]{0:T(1024)} %param.23) | copy-start | bytes 12292
  467.1 12.2 all-to-all-start
  471.4 88.2 %all-gather.12.cloned.1.call-start = ((), (), s32[]{:S(2)}) async-start(), calls=%async_computation.8 | async-start | bytes 2703360 | tf_op jit(solution)/shard_map/all_gather | solution.py:226
  482.4 2.1 copy-start.27
  482.4 2.1 copy-start.28
  484.5 3.1 copy-start.14
  484.5 2.0 copy-start.24
  485.4 0.8 copy-start.12
  487.1 516.8 %copy-start.25 = (f32[256]{0:T(256)}, f32[256]{0:T(256)S(1)}, u32[]{:S(2)}) copy-start(f32[256]{0:T(256)S(1)} %get-tuple-element.412) | copy-start | bytes 3076
  487.5 1.0 copy-start.18
  488.5 0.8 copy-start.16
  506.3 105.9 %all-gather.14.cloned.1.call-start = ((), (), s32[]{:S(2)}) async-start(), calls=%async_computation.9 | async-start | bytes 2703360 | tf_op jit(solution)/shard_map/all_gather | solution.py:226
  566.1 99.2 %all-gather.16.cloned.1.call-start = ((), (), s32[]{:S(2)}) async-start(), calls=%async_computation.10 | async-start | bytes 2703360 | tf_op jit(solution)/shard_map/all_gather | solution.py:226
  619.1 136.0 %all-gather.18.cloned.1.call-start = ((), (), s32[]{:S(2)}) async-start(), calls=%async_computation.11 | async-start | bytes 5406720 | tf_op jit(solution)/shard_map/all_gather | solution.py:230
  673.6 315.3 %reduce-scatter.11.cloned.1.call-start = ((), (), s32[]{:S(2)}) async-start(), calls=%async_computation.4 | async-start | bytes 4681728 | tf_op jit(solution)/shard_map/reduce_scatter | solution.py:241
  935.0 54.2 %copy-start.2 = (bf16[1040,256]{1,0:T(8,128)(2,1)S(1)}, bf16[1040,256]{1,0:T(8,128)(2,1)}, u32[]{:S(2)}) copy-start(bf16[1040,256]{1,0:T(8,128)(2,1)} %all_to_all.27) | copy-start | bytes 1597444
  935.0 54.2 %copy-start.17 = (bf16[256,1024]{1,0:T(8,128)(2,1)S(1)}, bf16[256,1024]{1,0:T(8,128)(2,1)}, u32[]{:S(2)}) copy-start(bf16[256,1024]{1,0:T(8,128)(2,1)} %copy-done.16) | copy-start | bytes 1572868
  935.1 128.4 %reduce-scatter.13.cloned.1.call-start = ((), (), s32[]{:S(2)}) async-start(), calls=%async_computation.7 | async-start | bytes 147456 | tf_op jit(solution)/shard_map/reduce_scatter | solution.py:242
  935.6 137.8 %all-gather.10.cloned.1.call-start = ((), (), s32[]{:S(2)}) async-start(), calls=%async_computation.5 | async-start | bytes 4681728 | tf_op jit(solution)/shard_map/all_gather | solution.py:245
  989.0 3.1 copy-start.15
  989.0 200.0 %all-reduce.17.cloned.1.call-start = ((), (), s32[]{:S(2)}) async-start(), calls=%async_computation.12 | async-start | bytes 16908288 | tf_op jit(solution)/shard_map/psum | solution.py:188
  989.3 2.8 copy-start.19
  994.9 1.2 copy-start.6
  994.9 272.8 %all-reduce.15.cloned.1.call-start = ((), (), s32[]{:S(2)}) async-start(), calls=%async_computation.6 | async-start | bytes 7299072 | tf_op jit(solution)/shard_map/psum | solution.py:239
  996.1 2.7 copy-start.3
  996.1 2.7 copy-start.10
  998.8 1.6 copy-start.4
  1003.9 1.6 copy-start.13
  1267.7 4.9 copy-start.11
  1272.6 3.5 copy-start.7
  1276.1 3.7 copy-start.8
  1279.9 3.1 copy-start.1
Sparse Core Ops, SparseCore 0:
  506.4 53.0 all-gather.11
  566.2 45.9 all-gather.13
  619.2 45.9 all-gather.15
  673.8 81.2 all-gather.17
  935.2 53.7 reduce-scatter.10
  992.7 34.1 reduce-scatter.12
  1028.7 38.2 all-gather.9
Sparse Core Ops, SparseCore 1:
  996.0 193.0 all-reduce.16
  1193.2 74.5 all-reduce.14
where the time goes:
time: 1300 us; the launch traced here: 1290 us
  waiting for transfers between devices  488 us (38%)
  blocking collectives  339 us (26%)
  local copies, waits for them, and re-layouts  237 us (18%)
  matrix products  135 us (10%)
  other arithmetic  55.1 us (4%)
  between operations  18 us (1%)
  starting transfers between devices  16.8 us (1%)
    unnamed x4, blocking collectives  261 us
    all_gather x3, waiting for transfers between devices, body(): lax.all_gather(mixed_grad, 'cross', axis=0, tiled=True)  145 us
    psum x1, waiting for transfers between devices, body(): lax.psum((loss_part, tower_one_grad, bias_one_grad, tower_two_grad, bias_...  116 us
    all_gather x1, waiting for transfers between devices, body(): full_grad = lax.all_gather(input_grad, 'cross', axis=0, tiled=True)  81.4 us
    psum x1, waiting for transfers between devices, body(): lax.psum((cross_pair[0], cross_pair[1]), 'dp')  78.7 us
    unnamed x77, local copies, waits for them, and re-layouts  53.6 us
    reduce_scatter x1, waiting for transfers between devices, body(): lax.psum_scatter(table_term, 'dp', scatter_dimension=0, tiled=True)  53.3 us
    dot_general x26, matrix products, lookup_add_field(): lax.dot_general(table_cols, hot_rows, contract_outer, preferred_element_t...  48.3 us
  transfers between devices with their start and end apart: 14, of which 11 were waited for; matrix products, arithmetic and copies ran while one was open for 2% of the time, Pallas kernels for 0%

commit v1 on v0

v1 whole, which is shorter than its diff:
```python
import functools

import jax
import jax.numpy as jnp
from jax import lax
from jax.experimental import pallas as pl
from jax.experimental.pallas import tpu as pltpu
from jax.sharding import PartitionSpec as P

F32 = jnp.float32
BF16 = jnp.bfloat16
ROWS_IN_ROWS = (((0,), (0,)), ((), ()))
LANES_IN_LANES = (((1,), (1,)), ((), ()))
LANES = 128
LOW_BITS = 8
LOW_ROWS = 1 << LOW_BITS
CHIPS = 4
MARGIN = 48
IN_VMEM = pl.BlockSpec(memory_space=pltpu.VMEM)
IN_SMEM = pl.BlockSpec(memory_space=pltpu.SMEM)
IN_PLACE = pl.BlockSpec(memory_space=pl.ANY)
Shape = jax.ShapeDtypeStruct


def round_up(size, step):
    return -(-size // step) * step


def dot(left, right, dims=(((1,), (0,)), ((), ()))):
    return lax.dot_general(left, right, dims, preferred_element_type=F32)


def silu_slope(pre_act):
    sigmoid_part = jax.nn.sigmoid(pre_act)
    return sigmoid_part * (1.0 + pre_act * (1.0 - sigmoid_part))


def params(mebibytes=56):
    return pltpu.CompilerParams(vmem_limit_bytes=mebibytes * 1024 * 1024)


def lookup_kernel(at, table, ids, *rest, fields, emb, ways):
    outs, gathered = rest[:ways], rest[ways]
    highs = table.shape[1] // LOW_ROWS
    group = ids.shape[1]
    part = group // ways
    slab = emb + 1
    low_iota = lax.broadcasted_iota(jnp.int32, (LOW_ROWS, group), 0)
    for field in range(fields):
        left = jnp.concatenate(
            [table[pl.ds(field * emb, slab), pl.ds(high * LOW_ROWS, LOW_ROWS)] for high in range(highs)], axis=0
        ).astype(BF16)
        local = ids[pl.ds(field, 1), :]
        low = jnp.bitwise_and(local, LOW_ROWS - 1)
        high_id = jnp.right_shift(local, LOW_BITS)
        hot = jnp.where(low_iota == low, 1.0, 0.0).astype(BF16)
        picked = dot(left, hot)
        total = jnp.zeros((slab, group), F32)
        for high in range(highs):
            total = total + jnp.where(high_id == high, picked[high * slab : (high + 1) * slab], 0.0)
        gathered[pl.ds(field * emb, slab), :] = total
    for step in range(ways):
        start = pl.multiple_of((at[0] ^ step) * part, part)
        outs[step][...] = gathered[:, pl.ds(start, part)].astype(BF16)


def count_kernel(ids, out, *, fields):
    highs = out.shape[1] // LOW_ROWS
    group = ids.shape[1]
    low_iota = lax.broadcasted_iota(jnp.int32, (LOW_ROWS, group), 0)
    high_iota = lax.broadcasted_iota(jnp.int32, (8, group), 0)
    for field in range(fields):
        local = ids[pl.ds(field, 1), :]
        low = jnp.bitwise_and(local, LOW_ROWS - 1)
        hot = jnp.where(low_iota == low, 1.0, 0.0).astype(BF16)
        marks = jnp.where(high_iota == jnp.right_shift(local, LOW_BITS), 1.0, 0.0).astype(BF16)
        got = dot(marks, hot, LANES_IN_LANES)
        for high in range(highs):
            out[pl.ds(field, 1), pl.ds(high * LOW_ROWS, LOW_ROWS)] = got[high : high + 1].astype(jnp.int32)


def weight_copies(own, pieces, weights, sems, at):
    ways, width = weights.shape[0], weights.shape[3]
    copies = [pltpu.make_async_copy(own.at[:, :, pl.ds(0, width)], weights.at[at[0]], sems.at[0])]
    for rel, piece in enumerate(pieces):
        column = pl.multiple_of(((at[1] ^ (rel // 2)) * 2 + (at[2] ^ (rel % 2))) * LANES, LANES)
        for step in range(1, ways):
            target = weights.at[at[0] ^ step, :, :, pl.ds(column, LANES)]
            copies.append(pltpu.make_async_copy(piece.at[step - 1], target, sems.at[len(copies)]))
    return copies


def split_cores(keep, send, core, value, chip_step, place_step, row):
    count = value.shape[0]
    first, second = value[:, :LANES], value[:, LANES:]
    keep[chip_step, place_step, pl.ds(row, count), :] = jnp.where(core == 0, first, second)
    send[chip_step, place_step, pl.ds(row, count), :] = jnp.where(core == 0, second, first).astype(BF16)


def forward_kernel(at, *refs, ways, emb_end, scale):
    refs = list(refs)
    take = lambda count: [refs.pop(0) for _ in range(count)]
    parts = take(ways)
    dense_t, own = take(2)
    pieces = take(2 * CHIPS)
    tails, bias, one_w, one_b, two_w, two_b, out_w, out_b, labels = take(9)
    first_out, lows, mixes, top_grad, logits_out, keep, send, small = take(8)
    weights, turned, first, state, sems = take(5)
    place, chip, core = at[0], at[1], at[2]
    layers, shard, full = own.shape
    rows = parts[0].shape[1]
    main = weights.shape[3]
    extra = full - main
    hidden = one_w.shape[1]
    copies = weight_copies(own, pieces, weights, sems, at)
    for copy in copies:
        copy.start()
    looked = parts[0][...].astype(F32)
    for piece in parts[1:]:
        looked = looked + piece[...].astype(F32)
    turned[pl.ds(0, looked.shape[0]), :] = looked
    turned[pl.ds(emb_end, dense_t.shape[0]), :] = dense_t[...]
    used = emb_end + dense_t.shape[0]
    turned[pl.ds(used, turned.shape[0] - used), :] = jnp.zeros((turned.shape[0] - used, rows), F32)
    start = turned[...].T[:, :full]
    first[...] = start
    state[...] = start
    first_out[...] = start.astype(BF16)
    for copy in copies:
        copy.wait()

    @pl.loop(0, layers)
    def _(layer):
        low = state[...].astype(BF16)
        lows[layer] = low
        body = jnp.zeros((rows, main), F32)
        edge = jnp.zeros((rows, extra), F32)
        for block in range(ways):
            chunk = low[:, shard * block : shard * (block + 1)]
            tail = tails[block, pl.ds(pl.multiple_of(extra * layer, extra), extra), pl.ds(0, shard)]
            body = body + dot(chunk, weights[block, layer])
            edge = edge + dot(chunk, tail, LANES_IN_LANES)
        mixed = jnp.concatenate([body, edge], axis=1) + bias[pl.ds(layer, 1), :]
        mixes[layer] = mixed
        state[...] = first[...] * mixed + state[...]

    top = state[...].astype(BF16)
    hid_one = dot(top, one_w[...]) + one_b[...]
    act_one = jax.nn.silu(hid_one).astype(BF16)
    hid_two = dot(act_one, two_w[...]) + two_b[...]
    act_two = jax.nn.silu(hid_two).astype(BF16)
    top_float, act_float = top.astype(F32), act_two.astype(F32)
    weight_top = out_w[:, :full].astype(F32)
    weight_act = out_w[:, full:].astype(F32)
    logits = (
        jnp.sum(top_float * weight_top, axis=1, keepdims=True)
        + jnp.sum(act_float * weight_act, axis=1, keepdims=True)
        + out_b[...]
    )
    logits_out[...] = logits
    label = labels[...]
    loss = jnp.sum(jax.nn.softplus(logits) - label * logits, axis=0, keepdims=True) * scale
    g_logit = ((jax.nn.sigmoid(logits) - label) * scale).astype(BF16).astype(F32)
    g_two = (g_logit * weight_act * silu_slope(hid_two)).astype(BF16)
    g_one = (dot(g_two, two_w[...], LANES_IN_LANES) * silu_slope(hid_one)).astype(BF16)
    top_grad[...] = (dot(g_one, one_w[...], LANES_IN_LANES) + g_logit * weight_top).astype(BF16)
    one_float, two_float = g_one.astype(F32), g_two.astype(F32)
    lane = lax.broadcasted_iota(jnp.int32, (1, LANES), 1)
    bias_grad = jnp.sum(g_logit, axis=0, keepdims=True)
    small[...] = jnp.zeros_like(small)
    small[pl.ds(0, 1), pl.ds(0, hidden)] = jnp.sum(one_float, axis=0, keepdims=True)
    small[pl.ds(1, 1), pl.ds(0, hidden)] = jnp.sum(two_float, axis=0, keepdims=True)
    small[pl.ds(2, 1), pl.ds(0, full)] = jnp.sum(top_float * g_logit, axis=0, keepdims=True)
    small[pl.ds(3, 1), pl.ds(0, hidden)] = jnp.sum(act_float * g_logit, axis=0, keepdims=True)
    small[pl.ds(7, 1), pl.ds(0, LANES)] = jnp.where(lane == 0, loss, jnp.where(lane == 1, bias_grad, 0.0))

    top_t = top_float.T
    tail_t = top_t[main:full].astype(BF16)
    top_t = top_t[:main].astype(BF16)
    act_t = act_one.astype(F32).T.astype(BF16)
    part = hidden // ways
    wide = 2 * LANES
    edge_rows = extra // ways
    state[:, :hidden] = one_float
    first[:, :hidden] = two_float
    for step in range(CHIPS):
        lanes = pl.ds(pl.multiple_of((chip ^ step) * wide, wide), wide)
        one_cols = state[:, lanes].astype(BF16)
        two_cols = first[:, lanes].astype(BF16)
        edge = dot(tail_t, one_cols)
        rest = keep.shape[2] - 2 * part
        for block in range(ways):
            target = place ^ block
            own_rows = slice(block * part, (block + 1) * part)
            split_cores(keep, send, core, dot(top_t[own_rows], one_cols), step, target, 0)
            split_cores(keep, send, core, dot(act_t[own_rows], two_cols), step, target, part)
            ends = edge[block * edge_rows : (block + 1) * edge_rows]
            ends = jnp.concatenate([ends, jnp.zeros((rest - edge_rows, wide), F32)], axis=0)
            split_cores(keep, send, core, ends, step, target, 2 * part)


def backward_kernel(at, *refs, ways, gap, dense_at):
    refs = list(refs)
    take = lambda count: [refs.pop(0) for _ in range(count)]
    (own,) = take(1)
    pieces = take(2 * CHIPS)
    tails, first_in, lows, mixes, top_grad = take(5)
    keep, send, emb_send, dense_grad, sums = take(5)
    weights, turned, g_mixed, low_t, pack, sems = take(6)
    place, chip, core = at[0], at[1], at[2]
    layers, shard, full = own.shape
    rows = first_in.shape[0]
    main = weights.shape[3]
    extra = full - main
    wide = 2 * LANES
    copies = weight_copies(own, pieces, weights, sems, at)
    for copy in copies:
        copy.start()
    pack[...] = jnp.zeros_like(pack)
    sums[...] = jnp.zeros_like(sums)
    first = first_in[...].astype(F32)
    grad = top_grad[...].astype(F32)
    total = jnp.zeros_like(grad)
    pad = jnp.zeros((rows, turned.shape[0] - full), F32)
    for copy in copies:
        copy.wait()
    for layer in reversed(range(layers)):
        rounded = (grad * first).astype(BF16)
        values = rounded.astype(F32)
        g_mixed[layer] = values[:, :main]
        sums[pl.ds(4 + layer, 1), pl.ds(0, full)] = jnp.sum(values, axis=0, keepdims=True)
        total = total + grad * mixes[layer]
        backs = []
        for block in range(ways):
            tail = tails[block, pl.ds(extra * layer, extra), pl.ds(0, shard)]
            backs.append(dot(rounded[:, :main], weights[block, layer], LANES_IN_LANES) + dot(rounded[:, main:full], tail))
        grad = grad + jnp.concatenate(backs, axis=1)
        low = lows[layer]
        edge = dot(rounded[:, main:full], low, ROWS_IN_ROWS)
        for block in range(ways):
            pack[block, :, pl.ds(layer * shard, shard)] = edge[:, block * shard : (block + 1) * shard]
        turned[...] = jnp.concatenate([low.astype(F32), pad], axis=1).T
        for block in range(ways):
            low_t[layer, block, pl.ds(0, shard), :] = turned[pl.ds(block * shard, shard), :].astype(BF16)
    total = total + grad
    dense_grad[...] = total[:, dense_at : dense_at + dense_grad.shape[1]]
    turned[...] = jnp.concatenate([total, pad], axis=1).T
    for step in range(CHIPS):
        emb_send[step ^ chip] = turned[pl.ds(step * wide, wide), :].astype(BF16)
    for step in range(CHIPS):
        lanes = pl.ds(pl.multiple_of((chip ^ step) * wide, wide), wide)
        for layer in range(layers):
            columns = g_mixed[layer, :, lanes].astype(BF16)
            for block in range(ways):
                product = dot(low_t[layer, block], columns)[:shard]
                product = jnp.concatenate([product, jnp.zeros((gap - shard, wide), F32)], axis=0)
                split_cores(keep, send, core, product, step, place ^ block, layer * gap)
        for block in range(ways):
            split_cores(keep, send, core, pack[block, :, lanes], step, place ^ block, layers * gap)


def scatter_kernel(at, *refs, ways, emb):
    pieces, ids, keep, send, spread, table = refs[:CHIPS], *refs[CHIPS:]
    place, chip, core = at[0], at[1], at[2]
    wide, part = pieces[0].shape
    group = part * CHIPS
    highs = table.shape[0]
    per = highs // ways
    half = per // 2
    slab = emb + 1
    spread[...] = jnp.zeros_like(spread)
    for step, piece in enumerate(pieces):
        spread[pl.ds(MARGIN, wide), pl.ds(step * part, part)] = piece[...].astype(F32)
    low_iota = lax.broadcasted_iota(jnp.int32, (LOW_ROWS, group), 0)
    for mine in range(CHIPS):

        @pl.when(chip == mine)
        def _(mine=mine):
            for slot in range(ids.shape[0]):
                begin = ((mine * wide) // emb + slot) * emb - mine * wide + MARGIN
                values = spread[pl.ds(begin, slab), :]
                this = ids[pl.ds(slot, 1), :]
                high_id = jnp.right_shift(this, LOW_BITS)
                hot = jnp.where(low_iota == jnp.bitwise_and(this, LOW_ROWS - 1), 1.0, 0.0).astype(BF16)
                stacked = jnp.concatenate(
                    [jnp.where(high_id == high, values, 0.0) for high in range(highs)], axis=0
                ).astype(BF16)
                got = dot(stacked, hot, LANES_IN_LANES)
                for high in range(highs):
                    table[high, pl.ds(begin, emb), :] = got[high * slab : high * slab + emb]

    for block in range(ways):
        target = block ^ place
        for piece in range(half):
            keep[target, piece] = table[block * per + core * half + piece, pl.ds(MARGIN, wide), :]
            send[target, piece] = table[block * per + (1 - core) * half + piece, pl.ds(MARGIN, wide), :].astype(BF16)


def turn_kernel(*refs):
    parts, out = refs[:-1], refs[-1]
    for piece in range(out.shape[0]):
        total = parts[0][piece].astype(F32)
        for part in parts[1:]:
            total = total + part[piece].astype(F32)
        out[piece] = total.T.astype(BF16)


def table_kernel(at, *refs):
    pieces, out = refs[:-1], refs[-1]
    half, low, wide = pieces[0].shape
    last = CHIPS - 1
    for rel, piece in enumerate(pieces):
        chip = at[1] ^ (rel // 2)
        core = at[2] ^ (rel % 2)
        for block in range(half):
            rows = pl.ds(pl.multiple_of(core * half * low + block * low, low), low)
            values = piece[block].astype(F32)

            @pl.when(chip < last)
            def _(rows=rows, values=values, chip=chip):
                out[rows, pl.ds(pl.multiple_of(chip * wide, wide), wide)] = values

            @pl.when(chip == last)
            def _(rows=rows, values=values):
                width = out.shape[1] - last * wide
                out[rows, pl.ds(last * wide, width)] = values[:, :width]


def tower_kernel(at, *refs, ways):
    pieces, (one_out, two_out) = refs[:-2], refs[-2:]
    hidden = two_out.shape[0]
    part = hidden // ways
    ends = (one_out.shape[0] - hidden) // ways
    for rel, piece in enumerate(pieces):
        column = pl.multiple_of(((at[1] ^ (rel // 2)) * 2 + (at[2] ^ (rel % 2))) * LANES, LANES)
        lanes = pl.ds(column, LANES)
        for block in range(ways):
            source = block ^ at[0]
            one_out[pl.ds(block * part, part), lanes] = piece[source, pl.ds(0, part), :].astype(F32)
            two_out[pl.ds(block * part, part), lanes] = piece[source, pl.ds(part, part), :].astype(F32)
            one_out[pl.ds(hidden + block * ends, ends), lanes] = piece[source, pl.ds(2 * part, ends), :].astype(F32)


def cross_kernel(at, *refs, gap):
    pieces, out, pack = refs[:-2], refs[-2], refs[-1]
    layers, shard, full = out.shape
    main = pack.shape[1]
    extra = full - main
    for rel, piece in enumerate(pieces):
        column = pl.multiple_of(((at[1] ^ (rel // 2)) * 2 + (at[2] ^ (rel % 2))) * LANES, LANES)
        lanes = pl.ds(column, LANES)
        for layer in range(layers):
            out[layer, :, lanes] = piece[pl.ds(layer * gap, shard), :].astype(F32)
        pack[pl.ds(0, extra), lanes] = piece[pl.ds(layers * gap, extra), :].astype(F32)
    pack[pl.ds(extra, pack.shape[0] - extra), :] = jnp.zeros((pack.shape[0] - extra, main), F32)
    turned = pack[...].T
    for layer in range(layers):
        out[layer, :, pl.ds(main, extra)] = turned[layer * shard : (layer + 1) * shard, :extra]


class Links:
    def __init__(self, dp_size, cross_size):
        bits = dp_size.bit_length() - 1
        axis_bits = (bits - 1) // 2
        self.dp_size, self.cross_size = dp_size, cross_size
        self.core = 1
        self.chip_masks = (1 << 1, 1 << (1 + axis_bits))
        used = (self.core, *self.chip_masks)
        self.others = tuple(1 << bit for bit in range(bits) if 1 << bit not in used)

    def chip_mask(self, step):
        return sum(mask for bit, mask in enumerate(self.chip_masks) if step >> bit & 1)

    def chip(self, dp_place):
        return sum((dp_place // mask % 2) << bit for bit, mask in enumerate(self.chip_masks))

    def over_dp(self, value, mask):
        return lax.ppermute(value, "dp", [(one, one ^ mask) for one in range(self.dp_size)])

    def over_cross(self, value, mask):
        return lax.ppermute(value, "cross", [(one, one ^ mask) for one in range(self.cross_size)])

    def chips_swap(self, value_of):
        return [self.over_dp(value_of(step), self.chip_mask(step)) for step in range(1, CHIPS)]

    def cross_swap(self, value_of):
        return [self.over_cross(value_of(step), step) for step in range(1, self.cross_size)]

    def add_others(self, value):
        for mask in self.others:
            value = value + self.over_dp(value.astype(BF16), mask).astype(F32)
        return value

    def everywhere(self, value):
        for bit in range(self.dp_size.bit_length() - 1):
            value = value + self.over_dp(value, 1 << bit)
        for bit in range(self.cross_size.bit_length() - 1):
            value = value + self.over_cross(value, 1 << bit)
        return value

    def plane_gather(self, value):
        by_chip = [value, *self.chips_swap(lambda step: value)]
        return [each for one in by_chip for each in (one, self.over_dp(one, self.core))]

    def scatter_sum(self, keep, send):
        held = keep + self.over_dp(send, self.core).astype(F32)
        got = self.chips_swap(lambda step: held[step].astype(BF16))
        held = held[0] + sum(one.astype(F32) for one in got)
        held = self.add_others(held)
        got = self.cross_swap(lambda step: held[step].astype(BF16))
        return held[0] + sum(one.astype(F32) for one in got)


def body(
    emb_table,
    dense_input,
    feature_ids,
    labels,
    cross_weight,
    cross_bias,
    tower_one,
    bias_one,
    tower_two,
    bias_two,
    out_weight,
    out_bias,
):
    layers, shard, full = cross_weight.shape
    group, fields = feature_ids.shape
    rows_here, emb_end = emb_table.shape
    emb = emb_end // fields
    dense_width = dense_input.shape[1]
    hidden = tower_one.shape[1]
    main = hidden
    extra = full - main
    ways = lax.axis_size("cross")
    place = lax.axis_index("cross")
    dp_place = lax.axis_index("dp")
    links = Links(lax.axis_size("dp"), ways)
    rows = group // ways
    scale = 1.0 / (group * links.dp_size)
    chip, core = links.chip(dp_place), dp_place % 2
    at = jnp.stack([place, chip, core]).astype(jnp.int32)
    wide = 2 * LANES
    gap = round_up(shard, 16)

    column = (chip * 2 + core) * LANES
    own_block = lax.dynamic_slice_in_dim(cross_weight, column, LANES, 2)
    foreign = jnp.stack(links.cross_swap(lambda step: own_block))
    pieces = links.plane_gather(foreign)
    tail = jnp.concatenate(
        [*(cross_weight[layer, :, main:].T for layer in range(layers)), cross_bias], axis=0
    )
    tail = jnp.pad(tail, ((0, round_up(tail.shape[0], 16) - tail.shape[0]), (0, round_up(shard, LANES) - shard)))
    tails = jnp.stack([tail, *links.cross_swap(lambda step: tail)])
    tails = jnp.stack([lax.dynamic_index_in_dim(tails, block ^ place, keepdims=False) for block in range(ways)])
    bias = jnp.concatenate(
        [tails[block, layers * extra : layers * extra + layers, :shard] for block in range(ways)], axis=1
    ).astype(F32)

    ids_t = feature_ids.T
    emb_rows = round_up(emb_end + 1, 8)
    table_t = jnp.pad(emb_table.T.astype(F32), ((0, emb_rows - emb_end), (0, 0)))
    local_ids = ids_t - place * rows_here
    looked = pl.pallas_call(
        functools.partial(lookup_kernel, fields=fields, emb=emb, ways=ways),
        out_shape=[Shape((emb_rows, rows), BF16)] * ways,
        in_specs=[IN_SMEM, IN_VMEM, IN_VMEM],
        out_specs=[IN_VMEM] * ways,
        scratch_shapes=[pltpu.VMEM((emb_rows, group), F32)],
        compiler_params=params(),
        name="lookup",
    )(at, table_t, local_ids)
    parts = [looked[0], *links.cross_swap(lambda step: looked[step])]

    own_ids = lax.dynamic_slice_in_dim(ids_t, place * rows, rows, 1)
    slots = max((one * wide + wide - 1) // emb - (one * wide) // emb + 1 for one in range(CHIPS))
    slot_ids = jnp.stack(
        [own_ids[jnp.array([min((one * wide) // emb + slot, fields - 1) for slot in range(slots)])] for one in range(CHIPS)]
    )
    ids_for = lambda step: lax.dynamic_index_in_dim(slot_ids, chip ^ step, keepdims=False)
    chip_ids = jnp.concatenate([ids_for(0), *links.chips_swap(ids_for)], axis=1)

    counted = pl.pallas_call(
        functools.partial(count_kernel, fields=fields),
        out_shape=Shape((fields, rows_here), jnp.int32),
        in_specs=[IN_VMEM],
        out_specs=IN_VMEM,
        compiler_params=params(),
        name="count",
    )(local_ids)
    for bit in range(links.dp_size.bit_length() - 1):
        counted = counted + links.over_dp(counted, 1 << bit)
    row_counts = counted.T

    own_dense = lax.dynamic_slice_in_dim(dense_input, place * rows, rows, 0)
    dense_t = jnp.pad(own_dense.T.astype(F32), ((0, round_up(dense_width, 8) - dense_width), (0, 0)))
    tower_rows = round_up(2 * (hidden // ways) + extra // ways, 16)
    turned_rows = round_up(full, LANES)
    weight_scratch = pltpu.VMEM((ways, layers, shard, main), BF16)
    copy_sems = pltpu.SemaphoreType.DMA((1 + 2 * CHIPS * (ways - 1),))
    first, lows, mixes, top_grad, logits, tower_keep, tower_send, small = pl.pallas_call(
        functools.partial(forward_kernel, ways=ways, emb_end=emb_end, scale=scale),
        out_shape=[
            Shape((rows, full), BF16),
            Shape((layers, rows, full), BF16),
            Shape((layers, rows, full), F32),
            Shape((rows, full), BF16),
            Shape((rows, 1), F32),
            Shape((CHIPS, ways, tower_rows, LANES), F32),
            Shape((CHIPS, ways, tower_rows, LANES), BF16),
            Shape((8, turned_rows), F32),
        ],
        in_specs=[IN_SMEM, *[IN_VMEM] * (ways + 1), *[IN_PLACE] * (1 + 2 * CHIPS), *[IN_VMEM] * 9],
        out_specs=[IN_VMEM] * 8,
        scratch_shapes=[
            weight_scratch,
            pltpu.VMEM((turned_rows, rows), F32),
            pltpu.VMEM((rows, full), F32),
            pltpu.VMEM((rows, full), F32),
            copy_sems,
        ],
        compiler_params=params(),
        name="forward",
    )(
        at,
        *parts,
        dense_t,
        cross_weight,
        *pieces,
        tails,
        bias,
        tower_one,
        bias_one[None, :],
        tower_two,
        bias_two[None, :],
        out_weight[None, :],
        out_bias[None, :],
        labels.astype(F32)[:, None],
    )
    tower_sum = links.scatter_sum(tower_keep, tower_send).astype(BF16)
    tower_all = jnp.stack([tower_sum, *links.cross_swap(lambda step: tower_sum)])
    tower_one_grad, tower_two_grad = pl.pallas_call(
        functools.partial(tower_kernel, ways=ways),
        out_shape=[Shape((full, hidden), F32), Shape((hidden, hidden), F32)],
        in_specs=[IN_SMEM, *[IN_VMEM] * (2 * CHIPS)],
        out_specs=[IN_VMEM] * 2,
        compiler_params=params(),
        name="towers",
    )(at, *links.plane_gather(tower_all))

    cross_rows = layers * gap + extra
    cross_keep, cross_send, emb_send, dense_grad, sums = pl.pallas_call(
        functools.partial(backward_kernel, ways=ways, gap=gap, dense_at=emb_end),
        out_shape=[
            Shape((CHIPS, ways, cross_rows, LANES), F32),
            Shape((CHIPS, ways, cross_rows, LANES), BF16),
            Shape((CHIPS, wide, rows), BF16),
            Shape((rows, dense_width), F32),
            Shape((8, turned_rows), F32),
        ],
        in_specs=[IN_SMEM, *[IN_PLACE] * (1 + 2 * CHIPS), *[IN_VMEM] * 5],
        out_specs=[IN_VMEM] * 5,
        scratch_shapes=[
            weight_scratch,
            pltpu.VMEM((turned_rows, rows), F32),
            pltpu.VMEM((layers, rows, main), F32),
            pltpu.VMEM((layers, ways, gap, rows), BF16),
            pltpu.VMEM((ways, extra, main), F32),
            copy_sems,
        ],
        compiler_params=params(),
        name="backward",
    )(at, cross_weight, *pieces, tails, first, lows, mixes, top_grad)

    half = rows_here // LOW_ROWS // 2
    emb_parts = [emb_send[0], *links.chips_swap(lambda step: emb_send[step])]
    table_keep, table_send = pl.pallas_call(
        functools.partial(scatter_kernel, ways=ways, emb=emb),
        out_shape=[Shape((ways, half, wide, LOW_ROWS), F32), Shape((ways, half, wide, LOW_ROWS), BF16)],
        in_specs=[IN_SMEM, *[IN_VMEM] * (CHIPS + 1)],
        out_specs=[IN_VMEM] * 2,
        scratch_shapes=[
            pltpu.VMEM((MARGIN + wide + 64, rows * CHIPS), F32),
            pltpu.VMEM((ways * 2 * half, MARGIN + wide + 64, LOW_ROWS), F32),
        ],
        compiler_params=params(),
        name="scatter",
    )(at, *emb_parts, chip_ids)
    held = table_keep + links.over_dp(table_send, links.core).astype(F32)
    held = links.add_others(held)
    got = links.cross_swap(lambda step: held[step].astype(BF16))
    turned = pl.pallas_call(
        turn_kernel,
        out_shape=Shape((half, LOW_ROWS, wide), BF16),
        in_specs=[IN_VMEM] * ways,
        out_specs=IN_VMEM,
        compiler_params=params(),
        name="turn",
    )(held[0], *got)
    table_grad = pl.pallas_call(
        table_kernel,
        out_shape=Shape((rows_here, emb_end), F32),
        in_specs=[IN_SMEM, *[IN_VMEM] * (2 * CHIPS)],
        out_specs=IN_VMEM,
        compiler_params=params(),
        name="table",
    )(at, *links.plane_gather(turned))

    cross_sum = links.scatter_sum(cross_keep, cross_send).astype(BF16)
    cross_weight_grad = pl.pallas_call(
        functools.partial(cross_kernel, gap=gap),
        out_shape=Shape((layers, shard, full), F32),
        in_specs=[IN_SMEM, *[IN_VMEM] * (2 * CHIPS)],
        out_specs=IN_VMEM,
        scratch_shapes=[pltpu.VMEM((LANES, main), F32)],
        compiler_params=params(),
        name="cross",
    )(at, *links.plane_gather(cross_sum))

    small = links.everywhere(small + sums)
    cross_bias_grad = lax.dynamic_slice_in_dim(small[4 : 4 + layers], place * shard, shard, 1)
    return (
        small[7, 0],
        logits[:, 0],
        dense_grad,
        table_grad,
        cross_weight_grad,
        cross_bias_grad,
        tower_one_grad,
        small[0, :hidden],
        tower_two_grad,
        small[1, :hidden],
        jnp.concatenate([small[2, :full], small[3, :hidden]]),
        small[7, 1:2],
        row_counts,
    )


def solution(mesh):
    in_specs = (
        P("cross", None),
        P("dp", None),
        P("dp", None),
        P(("dp", "cross")),
        P(None, "cross", None),
        P(None, "cross"),
        P(),
        P(),
        P(),
        P(),
        P(),
        P(),
    )
    out_specs = (
        P(),
        P(("dp", "cross")),
        P(("dp", "cross"), None),
        P("cross", None),
        P(None, "cross", None),
        P(None, "cross"),
        P(),
        P(),
        P(),
        P(),
        P(),
        P(),
        P("cross", None),
    )
    return jax.shard_map(body, mesh=mesh, in_specs=in_specs, out_specs=out_specs, check_vma=False)
```

time: 1300 us -> 400 us (0.31)
  blocking collectives: 339 us -> 0 us
  waiting for transfers between devices: 488 us -> 162 us
  local copies, waits for them, and re-layouts: 237 us -> 25.7 us
  matrix products: 135 us -> 0 us
  Pallas kernels: 0 us -> 74.2 us
  starting transfers between devices: 16.8 us -> 85.1 us
  other arithmetic: 55.1 us -> 31.4 us
    unnamed x4 -> x0, blocking collectives: 261 us -> none
    all_gather x5 -> x0, waiting for transfers between devices: 227 us -> none  [the longest x3 145 us: body(): lax.all_gather(mixed_grad, 'cross', axis=0, tiled=True)]
    psum x2 -> x0, waiting for transfers between devices: 194 us -> none  [the longest x1 116 us: body(): lax.psum((loss_part, tower_one_grad, bias_one_grad, tower_two_grad, bias_...]
    ppermute x0 -> x72, waiting for transfers between devices: none -> 162 us  [the longest x23 93.4 us: over_cross(): lax.ppermute(value, 'cross', [(one, one ^ mask) for one in range(self.cro...]
    dot_general x71 -> x0, matrix products: 135 us -> none  [the longest x26 48.3 us: lookup_add_field(): lax.dot_general(table_cols, hot_rows, contract_outer, preferred_element_t...]
    dynamic_update_slice x78 -> x0, local copies, waits for them, and re-layouts: 124 us -> none  [the longest x26 44.5 us: table_add_field(): lax.dynamic_update_slice_in_dim(grad_table, summed[:, :emb_width], field_...]
    ppermute x0 -> x72, starting transfers between devices: none -> 85.1 us  [the longest x49 61.5 us: over_dp(): lax.ppermute(value, 'dp', [(one, one ^ mask) for one in range(self.dp_siz...]
    pallas_call x0 -> x9, Pallas kernels: none -> 74.2 us  [the longest x1 20.6 us: body(): pl.pallas_call(functools.partial(forward_kernel, ways=ways, emb_end=emb_e...]
  transfers between devices with their start and end apart: 14 -> 72, of which waited for: 11 -> 27; matrix products, arithmetic and copies ran while one was open for 2% -> 13% of each run, Pallas kernels for 0% -> 13%
where the time goes in v1:
time: 400 us; the launch traced here: 393 us
  waiting for transfers between devices  162 us (40%)
  starting transfers between devices  85.1 us (21%)
  Pallas kernels  74.2 us (19%)
  other arithmetic  31.4 us (8%)
  local copies, waits for them, and re-layouts  25.7 us (6%)
  between operations  14.1 us (4%)
    ppermute x23, waiting for transfers between devices, over_cross(): lax.ppermute(value, 'cross', [(one, one ^ mask) for one in range(self.cro...  93.4 us
    ppermute x49, waiting for transfers between devices, over_dp(): lax.ppermute(value, 'dp', [(one, one ^ mask) for one in range(self.dp_siz...  68.9 us
    ppermute x49, starting transfers between devices, over_dp(): lax.ppermute(value, 'dp', [(one, one ^ mask) for one in range(self.dp_siz...  61.5 us
    ppermute x23, starting transfers between devices, over_cross(): lax.ppermute(value, 'cross', [(one, one ^ mask) for one in range(self.cro...  23.6 us
    pallas_call x1, Pallas kernels, body(): pl.pallas_call(functools.partial(forward_kernel, ways=ways, emb_end=emb_e...  20.6 us
    pallas_call x1, Pallas kernels, body(): pl.pallas_call(functools.partial(backward_kernel, ways=ways, gap=gap, den...  16.9 us
    another operation x5, other arithmetic  13.2 us
    unnamed x99, local copies, waits for them, and re-layouts  11.7 us
  transfers between devices with their start and end apart: 72, of which 27 were waited for; matrix products, arithmetic and copies ran while one was open for 13% of the time, Pallas kernels for 13%

profile of v1, /device:TPU:13, one launch (start us, length us, event | category | flops | bytes accessed | tf_op | source)
XLA Modules:
  0.0 392.8 jit_solution(1439698174214868124)
XLA Ops:
  2.1 2.3 collective-permute-start.4
  7.7 1.6 subtract_bitcast_fusion.ids
  9.3 4.0 %pad_convert_fusion.table = f32[1016,1024]{1,0:T(8,128)} fusion(bf16[1014,1024]{1,0:T(8,128)(2,1)} %bitcast.127), kind=kLoop, calls=%fused_computation.7 | loop fusion | flops 1040384 | bytes 6238208 | tf_op jit(solution)/shard_map/jit(_pad)/pad | solution.py:463
  13.3 8.5 %collective-permute-done.5 = bf16[3,260,128]{2,1,0:T(8,128)(2,1)S(1)} collective-permute-done((bf16[3,260,128]{2,1,0:T(8,128)(2,1)S(1)}, bf16[3,260,128]{2,1,0:T(8,128)(2,1)S(1)}, u32[]{:S(2)}, u32[]{:S(2)}) %collective-permute-start.5) | collective-permute-done | bytes 199712 | tf_op jit(solution)/shard_map/ppermute | solution.py:381
  22.2 2.2 collective-permute-start.11
  25.2 7.8 %lookup.1 = (bf16[1016,256]{1,0:T(8,128)(2,1)}, bf16[1016,256]{1,0:T(8,128)(2,1)}, bf16[1016,256]{1,0:T(8,128)(2,1)}, bf16[1016,256]{1,0:T(8,128)(2,1)}) custom-call(s32[3]{0:T(128)} %pad_add_fusion.2.at, f32[1016,1024]{1,0:T(8,128)} %pad_convert_fusion.table, s32[26,1024]{1,0:T(8,128)} %subtract_bitcast_fusion.ids), custom_call_target="tpu_custom_call" | custom-call | tf_op jit(solution)/shard_map/lookup/pallas_call | solution.py:465
  33.0 2.5 collective-permute-start.14
  35.5 10.2 %collective-permute-done.14 = bf16[64,384]{1,0:T(8,128)(2,1)S(1)} collective-permute-done((bf16[64,384]{1,0:T(8,128)(2,1)S(1)}, bf16[64,384]{1,0:T(8,128)(2,1)S(1)}, u32[]{:S(2)}, u32[]{:S(2)}) %collective-permute-start.14) | collective-permute-done | bytes 49184 | tf_op jit(solution)/shard_map/ppermute | solution.py:381
  45.9 3.2 collective-permute-done.15
  49.1 1.5 collective-permute-start.1
  50.6 9.4 %collective-permute-start.6 = (bf16[3,3,260,128]{3,2,1,0:T(8,128)(2,1)S(1)}, bf16[3,3,260,128]{3,2,1,0:T(8,128)(2,1)S(1)}, u32[]{:S(2)}, u32[]{:S(2)}) collective-permute-start(bf16[3,3,260,128]{3,2,1,0:T(8,128)(2,1)S(1)} %pad_maximum_fusion.refs_6_.refs_1_), channel_id=1, source_target_pairs={{0,4},{4,0},{8,12},{12,8},{16,20},{20,16},{24,28},{28,24},{1,5},{5... | collective-permute-start | bytes 1797128 | tf_op jit(solution)/shard_map/ppermute | solution.py:378
  60.6 11.0 %collective-permute-done.1.refs_2_ = bf16[1016,256]{1,0:T(8,128)(2,1)} collective-permute-done((bf16[1016,256]{1,0:T(8,128)(2,1)}, bf16[1016,256]{1,0:T(8,128)(2,1)}, u32[]{:S(2)}, u32[]{:S(2)}) %collective-permute-start.1) | collective-permute-done | bytes 520224 | tf_op jit(solution)/shard_map/ppermute | solution.py:381
  75.9 20.9 %collective-permute-done.2.refs_3_ = bf16[1016,256]{1,0:T(8,128)(2,1)} collective-permute-done((bf16[1016,256]{1,0:T(8,128)(2,1)}, bf16[1016,256]{1,0:T(8,128)(2,1)}, u32[]{:S(2)}, u32[]{:S(2)}) %collective-permute-start.2) | collective-permute-done | bytes 520224 | tf_op jit(solution)/shard_map/ppermute | solution.py:381
  97.6 20.6 %forward.1 = (bf16[256,1040]{1,0:T(8,128)(2,1)}, bf16[3,256,1040]{2,1,0:T(8,128)(2,1)}, f32[3,256,1040]{2,1,0:T(8,128)}, bf16[256,1040]{1,0:T(8,128)(2,1)}, f32[...) custom-call(s32[3]{0:T(128)} %pad_add_fusion.2.at, ...), custom_call_target="tpu_custom_call" | custom-call | tf_op jit(solution)/shard_map/forward/pallas_call | solution.py:502
  118.2 1.5 collective-permute-start.52
  119.7 16.9 %backward.1 = (f32[4,4,832,128]{3,2,1,0:T(8,128)}, bf16[4,4,832,128]{3,2,1,0:T(8,128)(2,1)}, bf16[4,256,256]{2,1,0:T(8,128)(2,1)}, f32[256,13]{1,0:T(8,128)}, f32[8,1152]{1,0:T(8,128)}) custom-call(s32[3]{0:T(128)} %pad_add_fusion.2.at, bf16[3,260,1040]{2,1,0:T(8,128)(2,1)} %refs_0_.1, bf16[3,3,260,128]{3,2,1,0:T(8,128)(2,1)} %copy-done.2, ...), custom_call_target="tpu_custom_call" | custom-call | tf_op jit(solution)/shard_map/backward/pallas_call | solution.py:553
  154.3 1.8 slice_bitcast_fusion.20
  159.9 1.8 collective-permute-done.22.refs_2_
  161.7 1.4 collective-permute-done.23.refs_3_
  163.7 7.1 %scatter.1 = (f32[4,2,256,256]{3,2,1,0:T(8,128)}, bf16[4,2,256,256]{3,2,1,0:T(8,128)(2,1)}) custom-call(s32[3]{0:T(128)} %pad_add_fusion.2.at, bf16[256,256]{1,0:T(8,128)(2,1)} %get-tuple-element.112.refs_0_, bf16[256,256]{1,0:T(8,128)(2,1)} %copy-done.33, bf16[256,256]{1,0:T(8,128)(2,1)} %copy-done.34, bf16[256,256]{1,0:T(8,128)(2,1)} %copy-done.35, ...), custom_call_target="tpu_custom_call" | custom-call | tf_op jit(solution)/shard_map/scatter/pallas_call | solution.py:578
  170.8 3.2 collective-permute-start.27
  174.0 5.2 %count.1 = s32[26,1024]{1,0:T(8,128)} custom-call(s32[26,1024]{1,0:T(8,128)} %subtract_bitcast_fusion.ids), custom_call_target="tpu_custom_call" | custom-call | tf_op jit(solution)/shard_map/count/pallas_call | solution.py:484
  181.7 1.4 collective-permute-start.70
  184.2 2.4 collective-permute-done.18
  188.0 1.4 collective-permute-done.19
  189.4 3.6 fusion.24
  194.0 1.8 collective-permute-start.55
  195.9 1.7 fusion.28
  198.5 4.9 %collective-permute-done.53 = bf16[4,528,128]{2,1,0:T(8,128)(2,1)S(1)} collective-permute-done((bf16[4,528,128]{2,1,0:T(8,128)(2,1)S(1)}, bf16[4,528,128]{2,1,0:T(8,128)(2,1)S(1)}, u32[]{:S(2)}, u32[]{:S(2)}) %collective-permute-start.53) | collective-permute-done | bytes 540704 | tf_op jit(solution)/shard_map/ppermute | solution.py:378
  203.4 1.5 collective-permute-start.20
  206.0 9.5 %collective-permute-done.55 = bf16[4,528,128]{2,1,0:T(8,128)(2,1)S(1)} collective-permute-done((bf16[4,528,128]{2,1,0:T(8,128)(2,1)S(1)}, bf16[4,528,128]{2,1,0:T(8,128)(2,1)S(1)}, u32[]{:S(2)}, u32[]{:S(2)}) %collective-permute-start.55) | collective-permute-done | bytes 540704 | tf_op jit(solution)/shard_map/ppermute | solution.py:378
  215.5 1.6 collective-permute-start.29
  219.1 4.1 %fusion.27 = (bf16[4,4,832,128]{3,2,1,0:T(8,128)(2,1)S(1)}, f32[4,4,832,128]{3,2,1,0:T(8,128)}) fusion(f32[4,4,832,128]{3,2,1,0:T(8,128)S(1)} %bitcast.126, bf16[4,4,832,128]{3,2,1,0:T(8,128)(2,1)S(1)} %collective-permute-done.38), kind=kLoop, calls=%fused_computation.91 | loop fusion | flops 5111808 | bytes 20447232 | tf_op jit(solution)/shard_map/convert.17
  223.2 2.0 collective-permute-start.56
  227.6 11.9 %collective-permute-done.29.refs_2_ = bf16[2,256,256]{2,1,0:T(8,128)(2,1)} collective-permute-done((bf16[2,256,256]{2,1,0:T(8,128)(2,1)}, bf16[2,256,256]{2,1,0:T(8,128)(2,1)}, u32[]{:S(2)}, u32[]{:S(2)}) %collective-permute-start.29) | collective-permute-done | bytes 262176 | tf_op jit(solution)/shard_map/ppermute | solution.py:381
  239.4 5.8 %collective-permute-done.30.refs_3_ = bf16[2,256,256]{2,1,0:T(8,128)(2,1)S(1)} collective-permute-done((bf16[2,256,256]{2,1,0:T(8,128)(2,1)}, bf16[2,256,256]{2,1,0:T(8,128)(2,1)S(1)}, u32[]{:S(2)}, u32[]{:S(2)}) %collective-permute-start.30) | collective-permute-done | bytes 262176 | tf_op jit(solution)/shard_map/ppermute | solution.py:381
  246.6 2.2 turn.1.refs_0_
  248.8 2.0 collective-permute-start.32
  252.6 28.8 %collective-permute-done.32.refs_2_ = bf16[2,256,256]{2,1,0:T(8,128)(2,1)S(1)} collective-permute-done((bf16[2,256,256]{2,1,0:T(8,128)(2,1)}, bf16[2,256,256]{2,1,0:T(8,128)(2,1)S(1)}, u32[]{:S(2)}, u32[]{:S(2)}) %collective-permute-start.32) | collective-permute-done | bytes 262176 | tf_op jit(solution)/shard_map/ppermute | solution.py:378
  281.4 4.3 %collective-permute-done.34.refs_4_ = bf16[2,256,256]{2,1,0:T(8,128)(2,1)S(1)} collective-permute-done((bf16[2,256,256]{2,1,0:T(8,128)(2,1)}, bf16[2,256,256]{2,1,0:T(8,128)(2,1)S(1)}, u32[]{:S(2)}, u32[]{:S(2)}) %collective-permute-start.34) | collective-permute-done | bytes 262176 | tf_op jit(solution)/shard_map/ppermute | solution.py:378
  285.7 4.4 %collective-permute-start.61 = (bf16[528,128]{1,0:T(8,128)(2,1)S(1)}, bf16[528,128]{1,0:T(8,128)(2,1)S(1)}, u32[]{:S(2)}, u32[]{:S(2)}) collective-permute-start(bf16[528,128]{1,0:T(8,128)(2,1)S(1)} %fusion.5), channel_id=1, source_target_pairs={{0,3},{1,2},{2,1},{3,0},{4,7},{5,6},{6,5},{7,4},{8,11},{9,10},{10,... | collective-permute-start | bytes 405512 | tf_op jit(solution)/shard_map/ppermute | solution.py:381
  290.1 1.8 collective-permute-done.60
  291.9 7.3 %collective-permute-done.61 = bf16[528,128]{1,0:T(8,128)(2,1)S(1)} collective-permute-done((bf16[528,128]{1,0:T(8,128)(2,1)S(1)}, bf16[528,128]{1,0:T(8,128)(2,1)S(1)}, u32[]{:S(2)}, u32[]{:S(2)}) %collective-permute-start.61) | collective-permute-done | bytes 135200 | tf_op jit(solution)/shard_map/ppermute | solution.py:381
  299.2 3.1 collective-permute-start.31
  303.4 3.9 collective-permute-start.33
  307.9 2.1 collective-permute-start.67
  310.0 2.6 fusion.25
  313.5 1.3 collective-permute-start.62
  314.8 6.0 %collective-permute-done.63.refs_2_ = bf16[4,528,128]{2,1,0:T(8,128)(2,1)S(1)} collective-permute-done((bf16[4,528,128]{2,1,0:T(8,128)(2,1)S(1)}, bf16[4,528,128]{2,1,0:T(8,128)(2,1)S(1)}, u32[]{:S(2)}, u32[]{:S(2)}) %collective-permute-start.63) | collective-permute-done | bytes 540704 | tf_op jit(solution)/shard_map/ppermute | solution.py:378
  320.8 2.2 collective-permute-start.64
  322.9 2.3 collective-permute-start.42
  326.9 1.6 add_bitcast_fusion
  328.5 1.6 copy.38
  330.1 1.6 reduce
  334.4 2.0 collective-permute-done.43
  337.4 9.5 %collective-permute-done.44 = bf16[832,128]{1,0:T(8,128)(2,1)S(1)} collective-permute-done((bf16[832,128]{1,0:T(8,128)(2,1)S(1)}, bf16[832,128]{1,0:T(8,128)(2,1)S(1)}, u32[]{:S(2)}, u32[]{:S(2)}) %collective-permute-start.44) | collective-permute-done | bytes 213024 | tf_op jit(solution)/shard_map/ppermute | solution.py:381
  346.9 1.8 collective-permute-start.68
  348.8 8.7 %collective-permute-start.46 = (bf16[832,128]{1,0:T(8,128)(2,1)S(1)}, bf16[832,128]{1,0:T(8,128)(2,1)S(1)}, u32[]{:S(2)}, u32[]{:S(2)}) collective-permute-start(bf16[832,128]{1,0:T(8,128)(2,1)S(1)} %fusion.3.refs_0_), channel_id=1, source_target_pairs={{0,8},{4,12},{8,0},{12,4},{16,24},{20,28},{24,16},{28,20},{1,9},{5... | collective-permute-start | bytes 638984 | tf_op jit(solution)/shard_map/ppermute | solution.py:378
  360.0 3.1 collective-permute-done.46.refs_2_
  363.9 4.7 %collective-permute-done.48.refs_4_ = bf16[832,128]{1,0:T(8,128)(2,1)S(1)} collective-permute-done((bf16[832,128]{1,0:T(8,128)(2,1)S(1)}, bf16[832,128]{1,0:T(8,128)(2,1)S(1)}, u32[]{:S(2)}, u32[]{:S(2)}) %collective-permute-start.48) | collective-permute-done | bytes 213024 | tf_op jit(solution)/shard_map/ppermute | solution.py:378
  371.1 4.0 %table.1 = f32[1024,1014]{1,0:T(8,128)} custom-call(s32[3]{0:T(128)} %pad_add_fusion.2.at, bf16[2,256,256]{2,1,0:T(8,128)(2,1)} %turn.1.refs_0_, bf16[2,256,256]{2,1,0:T(8,128)(2,1)} %collective-permute-done.31.refs_1_, bf16[2,256,256]{2,1,0:T(8,128)(2,1)} %copy-done.14, bf16[2,256,256]{2,1,0:T(8,128)(2,1)} %copy-done.16, bf16[2,256,256]{2,1,0:T(8,128)(2,1)} %copy-done.15, ...), custom_call_target="tpu_custom_call" | custom-call | tf_op jit(solution)/shard_map/table/pallas_call | solution.py:601
  375.1 5.3 %copy.39 = f32[1024,1014]{0,1:T(8,128)} copy(f32[1024,1014]{1,0:T(8,128)} %table.1) | data formatting | bytes 8306688
  380.5 6.8 %towers.1 = (f32[1040,1024]{1,0:T(8,128)}, f32[1024,1024]{1,0:T(8,128)}) custom-call(s32[3]{0:T(128)} %pad_add_fusion.2.at, bf16[4,528,128]{2,1,0:T(8,128)(2,1)} %copy-done.7, bf16[4,528,128]{2,1,0:T(8,128)(2,1)} %collective-permute-done.62.refs_1_, bf16[4,528,128]{2,1,0:T(8,128)(2,1)} %copy-done.11, bf16[4,528,128]{2,1,0:T(8,128)(2,1)} %collective-permute-done.64.refs_3_, ...), custom_call_target="tpu_custom_call" | custom-call | tf_op jit(solution)/shard_map/towers/pallas_call | solution.py:543
  388.8 3.6 cross.1
  (252 shorter events, 52.3 us)
Async XLA Ops:
  1.9 11.5 %collective-permute-start.3 = (bf16[3,260,128]{2,1,0:T(8,128)(2,1)S(1)}, bf16[3,260,128]{2,1,0:T(8,128)(2,1)S(1)}, u32[]{:S(2)}, u32[]{:S(2)}) collective-permute-start(bf16[3,260,128]{2,1,0:T(8,128)(2,1)S(1)} %constant_dynamic-slice_fusion.9), channel_id=1, source_target_pairs={{0,1},{1,0},{2,3},{3,2},{4,5},{5,4},{6,7},{7,6},{8,9},{9,8},{10,11... | collective-permute-start | bytes 599048 | tf_op jit(solution)/shard_map/ppermute | solution.py:381
  2.1 11.2 %collective-permute-start.4 = (bf16[3,260,128]{2,1,0:T(8,128)(2,1)S(1)}, bf16[3,260,128]{2,1,0:T(8,128)(2,1)S(1)}, u32[]{:S(2)}, u32[]{:S(2)}) collective-permute-start(bf16[3,260,128]{2,1,0:T(8,128)(2,1)S(1)} %constant_dynamic-slice_fusion.9), channel_id=1, source_target_pairs={{0,2},{1,3},{2,0},{3,1},{4,6},{5,7},{6,4},{7,5},{8,10},{9,11},{10,... | collective-permute-start | bytes 599048 | tf_op jit(solution)/shard_map/ppermute | solution.py:381
  4.4 17.4 %collective-permute-start.5 = (bf16[3,260,128]{2,1,0:T(8,128)(2,1)S(1)}, bf16[3,260,128]{2,1,0:T(8,128)(2,1)S(1)}, u32[]{:S(2)}, u32[]{:S(2)}) collective-permute-start(bf16[3,260,128]{2,1,0:T(8,128)(2,1)S(1)} %constant_dynamic-slice_fusion.9), channel_id=1, source_target_pairs={{0,3},{1,2},{2,1},{3,0},{4,7},{5,6},{6,5},{7,4},{8,11},{9,10},{10,... | collective-permute-start | bytes 599048 | tf_op jit(solution)/shard_map/ppermute | solution.py:381
  6.5 26.5 %collective-permute-start.13 = (bf16[64,384]{1,0:T(8,128)(2,1)S(1)}, bf16[64,384]{1,0:T(8,128)(2,1)S(1)}, u32[]{:S(2)}, u32[]{:S(2)}) collective-permute-start(bf16[64,384]{1,0:T(8,128)(2,1)S(1)} %fusion.14), channel_id=1, source_target_pairs={{0,1},{1,0},{2,3},{3,2},{4,5},{5,4},{6,7},{7,6},{8,9},{9,8},{10,11... | collective-permute-start | bytes 147464 | tf_op jit(solution)/shard_map/ppermute | solution.py:381
  21.9 38.1 %collective-permute-start.9 = (bf16[3,3,260,128]{3,2,1,0:T(8,128)(2,1)S(1)}, bf16[3,3,260,128]{3,2,1,0:T(8,128)(2,1)S(1)}, u32[]{:S(2)}, u32[]{:S(2)}) collective-permute-start(bf16[3,3,260,128]{3,2,1,0:T(8,128)(2,1)S(1)} %pad_maximum_fusion.refs_6_.refs_1_), channel_id=1, source_target_pairs={{0,16},{4,20},{8,24},{12,28},{16,0},{20,4},{24,8},{28,12},{1,17},{... | collective-permute-start | bytes 1797128 | tf_op jit(solution)/shard_map/ppermute | solution.py:378
  22.2 37.9 %collective-permute-start.11 = (bf16[3,3,260,128]{3,2,1,0:T(8,128)(2,1)S(1)}, bf16[3,3,260,128]{3,2,1,0:T(8,128)(2,1)S(1)}, u32[]{:S(2)}, u32[]{:S(2)}) collective-permute-start(bf16[3,3,260,128]{3,2,1,0:T(8,128)(2,1)S(1)} %pad_maximum_fusion.refs_6_.refs_1_), channel_id=1, source_target_pairs={{0,24},{4,28},{8,16},{12,20},{16,8},{20,12},{24,0},{28,4},{1,25},{... | collective-permute-start | bytes 1797128 | tf_op jit(solution)/shard_map/ppermute | solution.py:378
  24.3 36.2 %collective-permute-start.7 = (bf16[3,3,260,128]{3,2,1,0:T(8,128)(2,1)S(1)}, bf16[3,3,260,128]{3,2,1,0:T(8,128)(2,1)S(1)}, u32[]{:S(2)}, u32[]{:S(2)}) collective-permute-start(bf16[3,3,260,128]{3,2,1,0:T(8,128)(2,1)S(1)} %pad_maximum_fusion.refs_6_.refs_1_), channel_id=1, source_target_pairs={{0,8},{4,12},{8,0},{12,4},{16,24},{20,28},{24,16},{28,20},{1,9},{5... | collective-permute-start | bytes 1797128 | tf_op jit(solution)/shard_map/ppermute | solution.py:378
  33.0 17.6 %collective-permute-start = (bf16[1016,256]{1,0:T(8,128)(2,1)}, bf16[1016,256]{1,0:T(8,128)(2,1)}, u32[]{:S(2)}, u32[]{:S(2)}) collective-permute-start(bf16[1016,256]{1,0:T(8,128)(2,1)} %get-tuple-element.35), channel_id=1, source_target_pairs={{0,1},{1,0},{2,3},{3,2},{4,5},{5,4},{6,7},{7,6},{8,9},{9,8},{10,11... | collective-permute-start | bytes 1560584 | tf_op jit(solution)/shard_map/ppermute | solution.py:381
  33.0 12.6 %collective-permute-start.14 = (bf16[64,384]{1,0:T(8,128)(2,1)S(1)}, bf16[64,384]{1,0:T(8,128)(2,1)S(1)}, u32[]{:S(2)}, u32[]{:S(2)}) collective-permute-start(bf16[64,384]{1,0:T(8,128)(2,1)S(1)} %fusion.14), channel_id=1, source_target_pairs={{0,2},{1,3},{2,0},{3,1},{4,6},{5,7},{6,4},{7,5},{8,10},{9,11},{10,... | collective-permute-start | bytes 147464 | tf_op jit(solution)/shard_map/ppermute | solution.py:381
  49.1 22.6 %collective-permute-start.1 = (bf16[1016,256]{1,0:T(8,128)(2,1)}, bf16[1016,256]{1,0:T(8,128)(2,1)}, u32[]{:S(2)}, u32[]{:S(2)}) collective-permute-start(bf16[1016,256]{1,0:T(8,128)(2,1)} %get-tuple-element.36), channel_id=1, source_target_pairs={{0,2},{1,3},{2,0},{3,1},{4,6},{5,7},{6,4},{7,5},{8,10},{9,11},{10,... | collective-permute-start | bytes 1560584 | tf_op jit(solution)/shard_map/ppermute | solution.py:381
  50.6 46.2 %collective-permute-start.6 = (bf16[3,3,260,128]{3,2,1,0:T(8,128)(2,1)S(1)}, bf16[3,3,260,128]{3,2,1,0:T(8,128)(2,1)S(1)}, u32[]{:S(2)}, u32[]{:S(2)}) collective-permute-start(bf16[3,3,260,128]{3,2,1,0:T(8,128)(2,1)S(1)} %pad_maximum_fusion.refs_6_.refs_1_), channel_id=1, source_target_pairs={{0,4},{4,0},{8,12},{12,8},{16,20},{20,16},{24,28},{28,24},{1,5},{5... | collective-permute-start | bytes 1797128 | tf_op jit(solution)/shard_map/ppermute | solution.py:378
  60.0 36.8 %collective-permute-start.10 = (bf16[3,3,260,128]{3,2,1,0:T(8,128)(2,1)S(1)}, bf16[3,3,260,128]{3,2,1,0:T(8,128)(2,1)}, u32[]{:S(2)}, u32[]{:S(2)}) collective-permute-start(bf16[3,3,260,128]{3,2,1,0:T(8,128)(2,1)S(1)} %collective-permute-done.9.refs_10_.refs_5_), channel_id=1, source_target_pairs={{0,4},{4,0},{8,12},{12,8},{16,20},{20,16},{24,28},{28,24},{1,5},{5... | collective-permute-start | bytes 1797128 | tf_op jit(solution)/shard_map/ppermute | solution.py:378
  60.1 36.7 %collective-permute-start.12 = (bf16[3,3,260,128]{3,2,1,0:T(8,128)(2,1)S(1)}, bf16[3,3,260,128]{3,2,1,0:T(8,128)(2,1)}, u32[]{:S(2)}, u32[]{:S(2)}) collective-permute-start(bf16[3,3,260,128]{3,2,1,0:T(8,128)(2,1)S(1)} %collective-permute-done.11.refs_12_.refs_7_), channel_id=1, source_target_pairs={{0,4},{4,0},{8,12},{12,8},{16,20},{20,16},{24,28},{28,24},{1,5},{5... | collective-permute-start | bytes 1797128 | tf_op jit(solution)/shard_map/ppermute | solution.py:378
  60.5 36.3 %collective-permute-start.8 = (bf16[3,3,260,128]{3,2,1,0:T(8,128)(2,1)S(1)}, bf16[3,3,260,128]{3,2,1,0:T(8,128)(2,1)}, u32[]{:S(2)}, u32[]{:S(2)}) collective-permute-start(bf16[3,3,260,128]{3,2,1,0:T(8,128)(2,1)S(1)} %collective-permute-done.7.refs_8_.refs_3_), channel_id=1, source_target_pairs={{0,4},{4,0},{8,12},{12,8},{16,20},{20,16},{24,28},{28,24},{1,5},{5... | collective-permute-start | bytes 1797128 | tf_op jit(solution)/shard_map/ppermute | solution.py:378
  71.6 25.1 %collective-permute-start.2 = (bf16[1016,256]{1,0:T(8,128)(2,1)}, bf16[1016,256]{1,0:T(8,128)(2,1)}, u32[]{:S(2)}, u32[]{:S(2)}) collective-permute-start(bf16[1016,256]{1,0:T(8,128)(2,1)} %get-tuple-element.37), channel_id=1, source_target_pairs={{0,3},{1,2},{2,1},{3,0},{4,7},{5,6},{6,5},{7,4},{8,11},{9,10},{10,... | collective-permute-start | bytes 1560584 | tf_op jit(solution)/shard_map/ppermute | solution.py:381
  118.2 71.2 %collective-permute-start.52 = (bf16[4,4,528,128]{3,2,1,0:T(8,128)(2,1)}, bf16[4,4,528,128]{3,2,1,0:T(8,128)(2,1)}, u32[]{:S(2)}, u32[]{:S(2)}) collective-permute-start(bf16[4,4,528,128]{3,2,1,0:T(8,128)(2,1)} %get-tuple-element.52), channel_id=1, source_target_pairs={{0,4},{4,0},{8,12},{12,8},{16,20},{20,16},{24,28},{28,24},{1,5},{5... | collective-permute-start | bytes 6488072 | tf_op jit(solution)/shard_map/ppermute | solution.py:378
  136.6 82.5 %collective-permute-start.38 = (bf16[4,4,832,128]{3,2,1,0:T(8,128)(2,1)}, bf16[4,4,832,128]{3,2,1,0:T(8,128)(2,1)S(1)}, u32[]{:S(2)}, u32[]{:S(2)}) collective-permute-start(bf16[4,4,832,128]{3,2,1,0:T(8,128)(2,1)} %get-tuple-element.50), channel_id=1, source_target_pairs={{0,4},{4,0},{8,12},{12,8},{16,20},{20,16},{24,28},{28,24},{1,5},{5... | collective-permute-start | bytes 10223624 | tf_op jit(solution)/shard_map/ppermute | solution.py:378
  151.6 4.5 %collective-permute-start.24 = (s32[8,256]{1,0:T(8,128)S(1)}, s32[8,256]{1,0:T(8,128)S(1)}, u32[]{:S(2)}, u32[]{:S(2)}) collective-permute-start(s32[8,256]{1,0:T(8,128)S(1)} %get-tuple-element.129), channel_id=1, source_target_pairs={{0,8},{4,12},{8,0},{12,4},{16,24},{20,28},{24,16},{28,20},{1,9},{5... | collective-permute-start | bytes 24584 | tf_op jit(solution)/shard_map/ppermute | solution.py:378
  152.9 4.4 %collective-permute-start.25 = (s32[8,256]{1,0:T(8,128)S(1)}, s32[8,256]{1,0:T(8,128)S(1)}, u32[]{:S(2)}, u32[]{:S(2)}) collective-permute-start(s32[8,256]{1,0:T(8,128)S(1)} %get-tuple-element.128), channel_id=1, source_target_pairs={{0,16},{4,20},{8,24},{12,28},{16,0},{20,4},{24,8},{28,12},{1,17},{... | collective-permute-start | bytes 24584 | tf_op jit(solution)/shard_map/ppermute | solution.py:378
  153.1 4.4 %collective-permute-start.26 = (s32[8,256]{1,0:T(8,128)S(1)}, s32[8,256]{1,0:T(8,128)S(1)}, u32[]{:S(2)}, u32[]{:S(2)}) collective-permute-start(s32[8,256]{1,0:T(8,128)S(1)} %get-tuple-element.127), channel_id=1, source_target_pairs={{0,24},{4,28},{8,16},{12,20},{16,8},{20,12},{24,0},{28,4},{1,25},{... | collective-permute-start | bytes 24584 | tf_op jit(solution)/shard_map/ppermute | solution.py:378
  157.3 4.4 %collective-permute-start.22 = (bf16[256,256]{1,0:T(8,128)(2,1)S(1)}, bf16[256,256]{1,0:T(8,128)(2,1)S(1)}, u32[]{:S(2)}, u32[]{:S(2)}) collective-permute-start(bf16[256,256]{1,0:T(8,128)(2,1)S(1)} %get-tuple-element.110), channel_id=1, source_target_pairs={{0,16},{4,20},{8,24},{12,28},{16,0},{20,4},{24,8},{28,12},{1,17},{... | collective-permute-start | bytes 393224 | tf_op jit(solution)/shard_map/ppermute | solution.py:378
  157.5 5.5 %collective-permute-start.23 = (bf16[256,256]{1,0:T(8,128)(2,1)S(1)}, bf16[256,256]{1,0:T(8,128)(2,1)S(1)}, u32[]{:S(2)}, u32[]{:S(2)}) collective-permute-start(bf16[256,256]{1,0:T(8,128)(2,1)S(1)} %get-tuple-element.109), channel_id=1, source_target_pairs={{0,24},{4,28},{8,16},{12,20},{16,8},{20,12},{24,0},{28,4},{1,25},{... | collective-permute-start | bytes 393224 | tf_op jit(solution)/shard_map/ppermute | solution.py:378
  170.8 23.2 %collective-permute-start.27 = (bf16[4,2,256,256]{3,2,1,0:T(8,128)(2,1)}, bf16[4,2,256,256]{3,2,1,0:T(8,128)(2,1)S(1)}, u32[]{:S(2)}, u32[]{:S(2)}) collective-permute-start(bf16[4,2,256,256]{3,2,1,0:T(8,128)(2,1)} %get-tuple-element.48), channel_id=1, source_target_pairs={{0,4},{4,0},{8,12},{12,8},{16,20},{20,16},{24,28},{28,24},{1,5},{5... | collective-permute-start | bytes 3145736 | tf_op jit(solution)/shard_map/ppermute | solution.py:378
  181.7 4.9 %collective-permute-start.70 = (s32[26,1024]{1,0:T(8,128)S(1)}, s32[26,1024]{1,0:T(8,128)S(1)}, u32[]{:S(2)}, u32[]{:S(2)}) collective-permute-start(s32[26,1024]{1,0:T(8,128)S(1)} %add.185), channel_id=1, source_target_pairs={{0,8},{4,12},{8,0},{12,4},{16,24},{20,28},{24,16},{28,20},{1,9},{5... | collective-permute-start | bytes 319496 | tf_op jit(solution)/shard_map/ppermute | solution.py:378
  187.3 35.9 %collective-permute-start.71 = (s32[26,1024]{1,0:T(8,128)}, s32[26,1024]{1,0:T(8,128)}, u32[]{:S(2)}, u32[]{:S(2)}) collective-permute-start(s32[26,1024]{1,0:T(8,128)} %add.186), channel_id=1, source_target_pairs={{0,16},{4,20},{8,24},{12,28},{16,0},{20,4},{24,8},{28,12},{1,17},{... | collective-permute-start | bytes 319496 | tf_op jit(solution)/shard_map/ppermute | solution.py:378
  193.1 10.2 %collective-permute-start.53 = (bf16[4,528,128]{2,1,0:T(8,128)(2,1)S(1)}, bf16[4,528,128]{2,1,0:T(8,128)(2,1)S(1)}, u32[]{:S(2)}, u32[]{:S(2)}) collective-permute-start(bf16[4,528,128]{2,1,0:T(8,128)(2,1)S(1)} %get-tuple-element.94), channel_id=1, source_target_pairs={{0,8},{4,12},{8,0},{12,4},{16,24},{20,28},{24,16},{28,20},{1,9},{5... | collective-permute-start | bytes 1622024 | tf_op jit(solution)/shard_map/ppermute | solution.py:378
  193.2 11.7 %collective-permute-start.54 = (bf16[4,528,128]{2,1,0:T(8,128)(2,1)S(1)}, bf16[4,528,128]{2,1,0:T(8,128)(2,1)S(1)}, u32[]{:S(2)}, u32[]{:S(2)}) collective-permute-start(bf16[4,528,128]{2,1,0:T(8,128)(2,1)S(1)} %get-tuple-element.96), channel_id=1, source_target_pairs={{0,16},{4,20},{8,24},{12,28},{16,0},{20,4},{24,8},{28,12},{1,17},{... | collective-permute-start | bytes 1622024 | tf_op jit(solution)/shard_map/ppermute | solution.py:378
  194.0 21.5 %collective-permute-start.55 = (bf16[4,528,128]{2,1,0:T(8,128)(2,1)S(1)}, bf16[4,528,128]{2,1,0:T(8,128)(2,1)S(1)}, u32[]{:S(2)}, u32[]{:S(2)}) collective-permute-start(bf16[4,528,128]{2,1,0:T(8,128)(2,1)S(1)} %get-tuple-element.95), channel_id=1, source_target_pairs={{0,24},{4,28},{8,16},{12,20},{16,8},{20,12},{24,0},{28,4},{1,25},{... | collective-permute-start | bytes 1622024 | tf_op jit(solution)/shard_map/ppermute | solution.py:378
  203.4 22.0 %collective-permute-start.20 = (f32[8,1152]{1,0:T(8,128)S(1)}, f32[8,1152]{1,0:T(8,128)S(1)}, u32[]{:S(2)}, u32[]{:S(2)}) collective-permute-start(f32[8,1152]{1,0:T(8,128)S(1)} %add.159), channel_id=1, source_target_pairs={{0,2},{1,3},{2,0},{3,1},{4,6},{5,7},{6,4},{7,5},{8,10},{9,11},{10,... | collective-permute-start | bytes 110600 | tf_op jit(solution)/shard_map/ppermute | solution.py:381
  204.9 22.3 %collective-permute-start.28 = (bf16[2,256,256]{2,1,0:T(8,128)(2,1)}, bf16[2,256,256]{2,1,0:T(8,128)(2,1)}, u32[]{:S(2)}, u32[]{:S(2)}) collective-permute-start(bf16[2,256,256]{2,1,0:T(8,128)(2,1)} %get-tuple-element.102), channel_id=1, source_target_pairs={{0,1},{1,0},{2,3},{3,2},{4,5},{5,4},{6,7},{7,6},{8,9},{9,8},{10,11... | collective-permute-start | bytes 786440 | tf_op jit(solution)/shard_map/ppermute | solution.py:381
  215.5 23.9 %collective-permute-start.29 = (bf16[2,256,256]{2,1,0:T(8,128)(2,1)}, bf16[2,256,256]{2,1,0:T(8,128)(2,1)}, u32[]{:S(2)}, u32[]{:S(2)}) collective-permute-start(bf16[2,256,256]{2,1,0:T(8,128)(2,1)} %get-tuple-element.101), channel_id=1, source_target_pairs={{0,2},{1,3},{2,0},{3,1},{4,6},{5,7},{6,4},{7,5},{8,10},{9,11},{10,... | collective-permute-start | bytes 786440 | tf_op jit(solution)/shard_map/ppermute | solution.py:381
  219.1 26.1 %collective-permute-start.30 = (bf16[2,256,256]{2,1,0:T(8,128)(2,1)}, bf16[2,256,256]{2,1,0:T(8,128)(2,1)S(1)}, u32[]{:S(2)}, u32[]{:S(2)}) collective-permute-start(bf16[2,256,256]{2,1,0:T(8,128)(2,1)} %get-tuple-element.100), channel_id=1, source_target_pairs={{0,3},{1,2},{2,1},{3,0},{4,7},{5,6},{6,5},{7,4},{8,11},{9,10},{10,... | collective-permute-start | bytes 786440 | tf_op jit(solution)/shard_map/ppermute | solution.py:381
  223.2 22.6 %collective-permute-start.56 = (bf16[528,128]{1,0:T(8,128)(2,1)}, bf16[528,128]{1,0:T(8,128)(2,1)S(1)}, u32[]{:S(2)}, u32[]{:S(2)}) collective-permute-start(bf16[528,128]{1,0:T(8,128)(2,1)} %get-tuple-element.106), channel_id=1, source_target_pairs={{0,1},{1,0},{2,3},{3,2},{4,5},{5,4},{6,7},{7,6},{8,9},{9,8},{10,11... | collective-permute-start | bytes 405512 | tf_op jit(solution)/shard_map/ppermute | solution.py:381
  226.1 22.7 %collective-permute-start.57 = (bf16[528,128]{1,0:T(8,128)(2,1)S(1)}, bf16[528,128]{1,0:T(8,128)(2,1)S(1)}, u32[]{:S(2)}, u32[]{:S(2)}) collective-permute-start(bf16[528,128]{1,0:T(8,128)(2,1)S(1)} %copy-done.29), channel_id=1, source_target_pairs={{0,2},{1,3},{2,0},{3,1},{4,6},{5,7},{6,4},{7,5},{8,10},{9,11},{10,... | collective-permute-start | bytes 405512 | tf_op jit(solution)/shard_map/ppermute | solution.py:381
  227.2 23.7 %collective-permute-start.58 = (bf16[528,128]{1,0:T(8,128)(2,1)S(1)}, bf16[528,128]{1,0:T(8,128)(2,1)S(1)}, u32[]{:S(2)}, u32[]{:S(2)}) collective-permute-start(bf16[528,128]{1,0:T(8,128)(2,1)S(1)} %copy-done.28), channel_id=1, source_target_pairs={{0,3},{1,2},{2,1},{3,0},{4,7},{5,6},{6,5},{7,4},{8,11},{9,10},{10,... | collective-permute-start | bytes 405512 | tf_op jit(solution)/shard_map/ppermute | solution.py:381
  239.4 67.9 %collective-permute-start.39 = (bf16[4,832,128]{2,1,0:T(8,128)(2,1)S(1)}, bf16[4,832,128]{2,1,0:T(8,128)(2,1)}, u32[]{:S(2)}, u32[]{:S(2)}) collective-permute-start(bf16[4,832,128]{2,1,0:T(8,128)(2,1)S(1)} %get-tuple-element.91), channel_id=1, source_target_pairs={{0,8},{4,12},{8,0},{12,4},{16,24},{20,28},{24,16},{28,20},{1,9},{5... | collective-permute-start | bytes 2555912 | tf_op jit(solution)/shard_map/ppermute | solution.py:378
  245.2 62.2 %collective-permute-start.40 = (bf16[4,832,128]{2,1,0:T(8,128)(2,1)S(1)}, bf16[4,832,128]{2,1,0:T(8,128)(2,1)}, u32[]{:S(2)}, u32[]{:S(2)}) collective-permute-start(bf16[4,832,128]{2,1,0:T(8,128)(2,1)S(1)} %get-tuple-element.93), channel_id=1, source_target_pairs={{0,16},{4,20},{8,24},{12,28},{16,0},{20,4},{24,8},{28,12},{1,17},{... | collective-permute-start | bytes 2555912 | tf_op jit(solution)/shard_map/ppermute | solution.py:378
  245.8 62.1 %collective-permute-start.41 = (bf16[4,832,128]{2,1,0:T(8,128)(2,1)S(1)}, bf16[4,832,128]{2,1,0:T(8,128)(2,1)}, u32[]{:S(2)}, u32[]{:S(2)}) collective-permute-start(bf16[4,832,128]{2,1,0:T(8,128)(2,1)S(1)} %get-tuple-element.92), channel_id=1, source_target_pairs={{0,24},{4,28},{8,16},{12,20},{16,8},{20,12},{24,0},{28,4},{1,25},{... | collective-permute-start | bytes 2555912 | tf_op jit(solution)/shard_map/ppermute | solution.py:378
  248.8 32.6 %collective-permute-start.32 = (bf16[2,256,256]{2,1,0:T(8,128)(2,1)}, bf16[2,256,256]{2,1,0:T(8,128)(2,1)S(1)}, u32[]{:S(2)}, u32[]{:S(2)}) collective-permute-start(bf16[2,256,256]{2,1,0:T(8,128)(2,1)} %turn.1.refs_0_), channel_id=1, source_target_pairs={{0,8},{4,12},{8,0},{12,4},{16,24},{20,28},{24,16},{28,20},{1,9},{5... | collective-permute-start | bytes 786440 | tf_op jit(solution)/shard_map/ppermute | solution.py:378
  251.0 34.8 %collective-permute-start.34 = (bf16[2,256,256]{2,1,0:T(8,128)(2,1)}, bf16[2,256,256]{2,1,0:T(8,128)(2,1)S(1)}, u32[]{:S(2)}, u32[]{:S(2)}) collective-permute-start(bf16[2,256,256]{2,1,0:T(8,128)(2,1)} %turn.1.refs_0_), channel_id=1, source_target_pairs={{0,16},{4,20},{8,24},{12,28},{16,0},{20,4},{24,8},{28,12},{1,17},{... | collective-permute-start | bytes 786440 | tf_op jit(solution)/shard_map/ppermute | solution.py:378
  285.7 6.2 %collective-permute-start.60 = (bf16[528,128]{1,0:T(8,128)(2,1)S(1)}, bf16[528,128]{1,0:T(8,128)(2,1)S(1)}, u32[]{:S(2)}, u32[]{:S(2)}) collective-permute-start(bf16[528,128]{1,0:T(8,128)(2,1)S(1)} %fusion.5), channel_id=1, source_target_pairs={{0,2},{1,3},{2,0},{3,1},{4,6},{5,7},{6,4},{7,5},{8,10},{9,11},{10,... | collective-permute-start | bytes 405512 | tf_op jit(solution)/shard_map/ppermute | solution.py:381
  285.7 13.5 %collective-permute-start.61 = (bf16[528,128]{1,0:T(8,128)(2,1)S(1)}, bf16[528,128]{1,0:T(8,128)(2,1)S(1)}, u32[]{:S(2)}, u32[]{:S(2)}) collective-permute-start(bf16[528,128]{1,0:T(8,128)(2,1)S(1)} %fusion.5), channel_id=1, source_target_pairs={{0,3},{1,2},{2,1},{3,0},{4,7},{5,6},{6,5},{7,4},{8,11},{9,10},{10,... | collective-permute-start | bytes 405512 | tf_op jit(solution)/shard_map/ppermute | solution.py:381
  291.9 11.5 %collective-permute-start.36 = (bf16[2,256,256]{2,1,0:T(8,128)(2,1)}, bf16[2,256,256]{2,1,0:T(8,128)(2,1)}, u32[]{:S(2)}, u32[]{:S(2)}) collective-permute-start(bf16[2,256,256]{2,1,0:T(8,128)(2,1)} %turn.1.refs_0_), channel_id=1, source_target_pairs={{0,24},{4,28},{8,16},{12,20},{16,8},{20,12},{24,0},{28,4},{1,25},{... | collective-permute-start | bytes 786440 | tf_op jit(solution)/shard_map/ppermute | solution.py:378
  299.2 8.1 %collective-permute-start.31 = (bf16[2,256,256]{2,1,0:T(8,128)(2,1)}, bf16[2,256,256]{2,1,0:T(8,128)(2,1)}, u32[]{:S(2)}, u32[]{:S(2)}) collective-permute-start(bf16[2,256,256]{2,1,0:T(8,128)(2,1)} %turn.1.refs_0_), channel_id=1, source_target_pairs={{0,4},{4,0},{8,12},{12,8},{16,20},{20,16},{24,28},{28,24},{1,5},{5... | collective-permute-start | bytes 786440 | tf_op jit(solution)/shard_map/ppermute | solution.py:378
  303.4 10.0 %collective-permute-start.33 = (bf16[2,256,256]{2,1,0:T(8,128)(2,1)S(1)}, bf16[2,256,256]{2,1,0:T(8,128)(2,1)S(1)}, u32[]{:S(2)}, u32[]{:S(2)}) collective-permute-start(bf16[2,256,256]{2,1,0:T(8,128)(2,1)S(1)} %collective-permute-done.32.refs_2_), channel_id=1, source_target_pairs={{0,4},{4,0},{8,12},{12,8},{16,20},{20,16},{24,28},{28,24},{1,5},{5... | collective-permute-start | bytes 786440 | tf_op jit(solution)/shard_map/ppermute | solution.py:378
  307.3 15.7 %collective-permute-start.35 = (bf16[2,256,256]{2,1,0:T(8,128)(2,1)}, bf16[2,256,256]{2,1,0:T(8,128)(2,1)S(1)}, u32[]{:S(2)}, u32[]{:S(2)}) collective-permute-start(bf16[2,256,256]{2,1,0:T(8,128)(2,1)} %copy-done.15), channel_id=1, source_target_pairs={{0,4},{4,0},{8,12},{12,8},{16,20},{20,16},{24,28},{28,24},{1,5},{5... | collective-permute-start | bytes 786440 | tf_op jit(solution)/shard_map/ppermute | solution.py:378
  307.3 13.5 %collective-permute-start.63 = (bf16[4,528,128]{2,1,0:T(8,128)(2,1)S(1)}, bf16[4,528,128]{2,1,0:T(8,128)(2,1)S(1)}, u32[]{:S(2)}, u32[]{:S(2)}) collective-permute-start(bf16[4,528,128]{2,1,0:T(8,128)(2,1)S(1)} %pad_maximum_fusion.1.refs_0_), channel_id=1, source_target_pairs={{0,8},{4,12},{8,0},{12,4},{16,24},{20,28},{24,16},{28,20},{1,9},{5... | collective-permute-start | bytes 1622024 | tf_op jit(solution)/shard_map/ppermute | solution.py:378
  307.4 17.9 %collective-permute-start.65 = (bf16[4,528,128]{2,1,0:T(8,128)(2,1)S(1)}, bf16[4,528,128]{2,1,0:T(8,128)(2,1)S(1)}, u32[]{:S(2)}, u32[]{:S(2)}) collective-permute-start(bf16[4,528,128]{2,1,0:T(8,128)(2,1)S(1)} %pad_maximum_fusion.1.refs_0_), channel_id=1, source_target_pairs={{0,16},{4,20},{8,24},{12,28},{16,0},{20,4},{24,8},{28,12},{1,17},{... | collective-permute-start | bytes 1622024 | tf_op jit(solution)/shard_map/ppermute | solution.py:378
  307.9 24.7 %collective-permute-start.67 = (bf16[4,528,128]{2,1,0:T(8,128)(2,1)S(1)}, bf16[4,528,128]{2,1,0:T(8,128)(2,1)}, u32[]{:S(2)}, u32[]{:S(2)}) collective-permute-start(bf16[4,528,128]{2,1,0:T(8,128)(2,1)S(1)} %pad_maximum_fusion.1.refs_0_), channel_id=1, source_target_pairs={{0,24},{4,28},{8,16},{12,20},{16,8},{20,12},{24,0},{28,4},{1,25},{... | collective-permute-start | bytes 1622024 | tf_op jit(solution)/shard_map/ppermute | solution.py:378
  313.5 44.0 %collective-permute-start.62 = (bf16[4,528,128]{2,1,0:T(8,128)(2,1)S(1)}, bf16[4,528,128]{2,1,0:T(8,128)(2,1)}, u32[]{:S(2)}, u32[]{:S(2)}) collective-permute-start(bf16[4,528,128]{2,1,0:T(8,128)(2,1)S(1)} %pad_maximum_fusion.1.refs_0_), channel_id=1, source_target_pairs={{0,4},{4,0},{8,12},{12,8},{16,20},{20,16},{24,28},{28,24},{1,5},{5... | collective-permute-start | bytes 1622024 | tf_op jit(solution)/shard_map/ppermute | solution.py:378
  320.8 36.7 %collective-permute-start.64 = (bf16[4,528,128]{2,1,0:T(8,128)(2,1)S(1)}, bf16[4,528,128]{2,1,0:T(8,128)(2,1)}, u32[]{:S(2)}, u32[]{:S(2)}) collective-permute-start(bf16[4,528,128]{2,1,0:T(8,128)(2,1)S(1)} %collective-permute-done.63.refs_2_), channel_id=1, source_target_pairs={{0,4},{4,0},{8,12},{12,8},{16,20},{20,16},{24,28},{28,24},{1,5},{5... | collective-permute-start | bytes 1622024 | tf_op jit(solution)/shard_map/ppermute | solution.py:378
  322.9 11.0 %collective-permute-start.42 = (bf16[832,128]{1,0:T(8,128)(2,1)}, bf16[832,128]{1,0:T(8,128)(2,1)S(1)}, u32[]{:S(2)}, u32[]{:S(2)}) collective-permute-start(bf16[832,128]{1,0:T(8,128)(2,1)} %get-tuple-element.103), channel_id=1, source_target_pairs={{0,1},{1,0},{2,3},{3,2},{4,5},{5,4},{6,7},{7,6},{8,9},{9,8},{10,11... | collective-permute-start | bytes 638984 | tf_op jit(solution)/shard_map/ppermute | solution.py:381
  326.1 10.3 %collective-permute-start.43 = (bf16[832,128]{1,0:T(8,128)(2,1)}, bf16[832,128]{1,0:T(8,128)(2,1)S(1)}, u32[]{:S(2)}, u32[]{:S(2)}) collective-permute-start(bf16[832,128]{1,0:T(8,128)(2,1)} %get-tuple-element.105), channel_id=1, source_target_pairs={{0,2},{1,3},{2,0},{3,1},{4,6},{5,7},{6,4},{7,5},{8,10},{9,11},{10,... | collective-permute-start | bytes 638984 | tf_op jit(solution)/shard_map/ppermute | solution.py:381
  332.7 16.1 %collective-permute-start.37 = (bf16[2,256,256]{2,1,0:T(8,128)(2,1)}, bf16[2,256,256]{2,1,0:T(8,128)(2,1)S(1)}, u32[]{:S(2)}, u32[]{:S(2)}) collective-permute-start(bf16[2,256,256]{2,1,0:T(8,128)(2,1)} %collective-permute-done.36.refs_6_), channel_id=1, source_target_pairs={{0,4},{4,0},{8,12},{12,8},{16,20},{20,16},{24,28},{28,24},{1,5},{5... | collective-permute-start | bytes 786440 | tf_op jit(solution)/shard_map/ppermute | solution.py:378
  334.0 25.5 %collective-permute-start.66 = (bf16[4,528,128]{2,1,0:T(8,128)(2,1)}, bf16[4,528,128]{2,1,0:T(8,128)(2,1)S(1)}, u32[]{:S(2)}, u32[]{:S(2)}) collective-permute-start(bf16[4,528,128]{2,1,0:T(8,128)(2,1)} %copy-done.12), channel_id=1, source_target_pairs={{0,4},{4,0},{8,12},{12,8},{16,20},{20,16},{24,28},{28,24},{1,5},{5... | collective-permute-start | bytes 1622024 | tf_op jit(solution)/shard_map/ppermute | solution.py:378
  336.4 10.5 %collective-permute-start.44 = (bf16[832,128]{1,0:T(8,128)(2,1)S(1)}, bf16[832,128]{1,0:T(8,128)(2,1)S(1)}, u32[]{:S(2)}, u32[]{:S(2)}) collective-permute-start(bf16[832,128]{1,0:T(8,128)(2,1)S(1)} %get-tuple-element.104), channel_id=1, source_target_pairs={{0,3},{1,2},{2,1},{3,0},{4,7},{5,6},{6,5},{7,4},{8,11},{9,10},{10,... | collective-permute-start | bytes 638984 | tf_op jit(solution)/shard_map/ppermute | solution.py:381
  346.9 33.6 %collective-permute-start.68 = (bf16[4,528,128]{2,1,0:T(8,128)(2,1)}, bf16[4,528,128]{2,1,0:T(8,128)(2,1)}, u32[]{:S(2)}, u32[]{:S(2)}) collective-permute-start(bf16[4,528,128]{2,1,0:T(8,128)(2,1)} %collective-permute-done.67.refs_6_), channel_id=1, source_target_pairs={{0,4},{4,0},{8,12},{12,8},{16,20},{20,16},{24,28},{28,24},{1,5},{5... | collective-permute-start | bytes 1622024 | tf_op jit(solution)/shard_map/ppermute | solution.py:378
  348.8 14.3 %collective-permute-start.46 = (bf16[832,128]{1,0:T(8,128)(2,1)S(1)}, bf16[832,128]{1,0:T(8,128)(2,1)S(1)}, u32[]{:S(2)}, u32[]{:S(2)}) collective-permute-start(bf16[832,128]{1,0:T(8,128)(2,1)S(1)} %fusion.3.refs_0_), channel_id=1, source_target_pairs={{0,8},{4,12},{8,0},{12,4},{16,24},{20,28},{24,16},{28,20},{1,9},{5... | collective-permute-start | bytes 638984 | tf_op jit(solution)/shard_map/ppermute | solution.py:378
  357.5 11.1 %collective-permute-start.48 = (bf16[832,128]{1,0:T(8,128)(2,1)S(1)}, bf16[832,128]{1,0:T(8,128)(2,1)S(1)}, u32[]{:S(2)}, u32[]{:S(2)}) collective-permute-start(bf16[832,128]{1,0:T(8,128)(2,1)S(1)} %fusion.3.refs_0_), channel_id=1, source_target_pairs={{0,16},{4,20},{8,24},{12,28},{16,0},{20,4},{24,8},{28,12},{1,17},{... | collective-permute-start | bytes 638984 | tf_op jit(solution)/shard_map/ppermute | solution.py:378
  357.5 12.2 %collective-permute-start.50 = (bf16[832,128]{1,0:T(8,128)(2,1)S(1)}, bf16[832,128]{1,0:T(8,128)(2,1)S(1)}, u32[]{:S(2)}, u32[]{:S(2)}) collective-permute-start(bf16[832,128]{1,0:T(8,128)(2,1)S(1)} %fusion.3.refs_0_), channel_id=1, source_target_pairs={{0,24},{4,28},{8,16},{12,20},{16,8},{20,12},{24,0},{28,4},{1,25},{... | collective-permute-start | bytes 638984 | tf_op jit(solution)/shard_map/ppermute | solution.py:378
  359.5 27.8 %collective-permute-start.45 = (bf16[832,128]{1,0:T(8,128)(2,1)S(1)}, bf16[832,128]{1,0:T(8,128)(2,1)S(1)}, u32[]{:S(2)}, u32[]{:S(2)}) collective-permute-start(bf16[832,128]{1,0:T(8,128)(2,1)S(1)} %fusion.3.refs_0_), channel_id=1, source_target_pairs={{0,4},{4,0},{8,12},{12,8},{16,20},{20,16},{24,28},{28,24},{1,5},{5... | collective-permute-start | bytes 638984 | tf_op jit(solution)/shard_map/ppermute | solution.py:378
  363.1 24.1 %collective-permute-start.47 = (bf16[832,128]{1,0:T(8,128)(2,1)S(1)}, bf16[832,128]{1,0:T(8,128)(2,1)S(1)}, u32[]{:S(2)}, u32[]{:S(2)}) collective-permute-start(bf16[832,128]{1,0:T(8,128)(2,1)S(1)} %collective-permute-done.46.refs_2_), channel_id=1, source_target_pairs={{0,4},{4,0},{8,12},{12,8},{16,20},{20,16},{24,28},{28,24},{1,5},{5... | collective-permute-start | bytes 638984 | tf_op jit(solution)/shard_map/ppermute | solution.py:378
  368.6 18.6 %collective-permute-start.49 = (bf16[832,128]{1,0:T(8,128)(2,1)S(1)}, bf16[832,128]{1,0:T(8,128)(2,1)S(1)}, u32[]{:S(2)}, u32[]{:S(2)}) collective-permute-start(bf16[832,128]{1,0:T(8,128)(2,1)S(1)} %collective-permute-done.48.refs_4_), channel_id=1, source_target_pairs={{0,4},{4,0},{8,12},{12,8},{16,20},{20,16},{24,28},{28,24},{1,5},{5... | collective-permute-start | bytes 638984 | tf_op jit(solution)/shard_map/ppermute | solution.py:378
  369.7 17.5 %collective-permute-start.51 = (bf16[832,128]{1,0:T(8,128)(2,1)S(1)}, bf16[832,128]{1,0:T(8,128)(2,1)S(1)}, u32[]{:S(2)}, u32[]{:S(2)}) collective-permute-start(bf16[832,128]{1,0:T(8,128)(2,1)S(1)} %collective-permute-done.50.refs_6_), channel_id=1, source_target_pairs={{0,4},{4,0},{8,12},{12,8},{16,20},{20,16},{24,28},{28,24},{1,5},{5... | collective-permute-start | bytes 638984 | tf_op jit(solution)/shard_map/ppermute | solution.py:378
  (55 other events, 863.5 us)
